TPU v7x, 128 devices: a whole 4x4x4 slice. The times are simulated.
128 devices in a mesh: dp: 8 (over x, core), tensor: 16 (over z, y).
Axes of the slice: x: 4, y: 4, z: 4, core: 2. Of those that a mesh axis runs over, the one named last changes fastest.
Arguments:
- hidden: bfloat16 [2, 2048, 5120], P(None, 'dp', 'tensor'), may hold values from -48 to 48
- draft_head: bfloat16 [5120, 24000], P(None, 'tensor'), may hold values from -0.09782797 to 0.09782797
- target_logits: bfloat16 [2048, 151936], P('dp', 'tensor'), may hold values from -320 to 320
- draft_to_target: int32 [24000], replicated, may hold values from 0 to 151935, as said below
Outputs:
- grad_hidden: bfloat16 [2, 2048, 5120], P(None, 'dp', 'tensor')
- grad_head: float32 [5120, 24000], P('dp', 'tensor')
Inputs may be any that keep to these rules, and one draw needn't show every extreme that they name: `draft_to_target`: all ids are distinct. Of the 1500 draft ids of one aligned block, at most 270 lie in any one aligned block of 9496 target ids, and in every draft block exactly 270 lie in one target block.
All inputs are finite; a program needn't handle non-finite values.
Results may differ from a plain program's by a relative error of at most 0.0054.
Values may be sent and summed in bfloat16 or wider, within the bound.
A program may use at most 192 MiB of HBM per device.

v0:
```python
import jax
import jax.numpy as jnp
from jax import lax
from jax.sharding import PartitionSpec as P

LOSS_SCALE = 256.0
STEP_DECAY = 0.8


def per_device(hidden, draft_head, target_logits, draft_to_target):
    parts = lax.axis_size("tensor")
    mine = lax.axis_index("tensor")
    dshard = draft_head.shape[1]
    tshard = target_logits.shape[1]
    block = draft_to_target.shape[0] // parts
    heavy = block // 8
    bound = heavy + (block - heavy + parts - 1) // parts
    owner_grid = (draft_to_target // tshard).reshape(parts, block)
    local_grid = (draft_to_target % tshard).reshape(parts, block)
    hits = (owner_grid[:, :, None] == jnp.arange(parts, dtype=jnp.int32)[None, None, :]).astype(
        jnp.int32
    )
    slot_grid = jnp.sum(jnp.cumsum(hits, axis=1) * hits, axis=2) - 1
    flat_slot = jnp.arange(parts, dtype=jnp.int32)[:, None] * bound + slot_grid
    placing = jnp.where(owner_grid == mine, flat_slot, parts * bound)
    table = (
        jnp.zeros((parts * bound,), jnp.int32)
        .at[placing.reshape(-1)]
        .set(local_grid.reshape(-1), mode="drop")
    )
    h_full = lax.all_gather(hidden, "tensor", axis=2, tiled=True)
    scores = jnp.einsum("std,dv->stv", h_full, draft_head, preferred_element_type=jnp.float32)
    logits = target_logits.astype(jnp.float32)
    tpeak_local = jnp.max(logits, axis=1)
    dpeak_local = jnp.max(scores, axis=2)
    tpeak, dpeak = lax.pmax((tpeak_local, dpeak_local), "tensor")
    ttotal, dtotal = lax.psum(
        (
            jnp.sum(jnp.exp(logits - tpeak[:, None]), axis=1),
            jnp.sum(jnp.exp(scores - dpeak[..., None]), axis=2),
        ),
        "tensor",
    )
    owned_probs = (jnp.exp(logits - tpeak[:, None]) / ttotal[:, None]).astype(jnp.bfloat16)
    outgoing = jnp.take(owned_probs, table, axis=1)
    incoming = lax.all_to_all(outgoing, "tensor", split_axis=1, concat_axis=1, tiled=True)
    my_owner = lax.dynamic_index_in_dim(owner_grid, mine, 0, keepdims=False)
    my_slot = lax.dynamic_index_in_dim(slot_grid, mine, 0, keepdims=False)
    probs = jnp.take(incoming, my_owner * bound + my_slot, axis=1)
    mass = lax.psum(jnp.sum(probs.astype(jnp.float32), axis=1), "tensor")
    soft = jnp.exp(scores - dpeak[..., None]) / dtotal[..., None]
    slope_list = []
    for step in range(hidden.shape[0]):
        shifted = jnp.concatenate([probs[step:], jnp.zeros((step, dshard), jnp.bfloat16)], axis=0)
        shifted_mass = jnp.concatenate([mass[step:], jnp.zeros((step,), jnp.float32)], axis=0)
        slope_list.append(
            (
                LOSS_SCALE
                * STEP_DECAY**step
                * (soft[step] * shifted_mass[:, None] - shifted.astype(jnp.float32))
            ).astype(jnp.bfloat16)
        )
    slopes = jnp.stack(slope_list)
    terms = jnp.einsum("stv,dv->std", slopes, draft_head, preferred_element_type=jnp.float32)
    grad_hidden = lax.psum_scatter(terms, "tensor", scatter_dimension=2, tiled=True).astype(
        jnp.bfloat16
    )
    grad_head = lax.psum_scatter(
        jnp.einsum("stc,stv->cv", h_full, slopes, preferred_element_type=jnp.float32),
        "dp",
        scatter_dimension=0,
        tiled=True,
    )
    return (grad_hidden, grad_head)


def solution(mesh):
    in_specs = (P(None, "dp", "tensor"), P(None, "tensor"), P("dp", "tensor"), P())
    out_specs = (P(None, "dp", "tensor"), P("dp", "tensor"))
    return jax.shard_map(
        per_device, mesh=mesh, in_specs=in_specs, out_specs=out_specs, check_vma=False
    )
```

profile of v0, /device:TPU:1, one launch (start us, length us, event | category | flops | bytes accessed | tf_op | source)
XLA Modules:
  0.0 721.4 jit_solution(9294487498048871753)
XLA Ops:
  7.2 0.0 all-gather.2.cloned.1.call-start
  7.2 0.7 all-gather.2.cloned.1.call-update
  7.9 1.0 add_select_fusion.1
  8.9 0.1 reshape.127
  9.0 0.2 iota_compare_fusion
  9.2 0.2 pad_convert_fusion
  9.4 1.6 reshape.130
  11.0 125.2 %reduce-window.6 = s32[16,16,12,128]{3,2,1,0:T(8,128)S(1)} reduce-window(s32[16,16,12,128]{3,2,1,0:T(8,128)} %reshape.130, s32[]{:T(128)} %constant.74.clone.1), window={size=1x1x1x128 pad=0_0x0_0x0_0x127_0}, to_apply=%region_4.5 | reduce-window | flops 49938432 | bytes 3145732 | tf_op jit(solution)/shard_map/reduce-window
  136.2 1.9 slice.33
  138.1 2.8 copy.6
  140.9 0.5 fusion.16
  141.4 0.2 copy.7
  141.6 1.7 broadcast_add_fusion
  143.3 0.0 copy-start.1
  143.3 1.7 reduce_window_sum.16
  145.0 0.4 fusion.7
  145.4 0.1 broadcast_add_fusion.2
  145.4 0.1 add.97
  145.6 0.0 copy-done.1
  145.6 0.1 add_select_fusion
  145.7 110.7 %scatter_custom_fusion = s32[4320]{0:T(1024)S(1)} fusion(s32[24000]{0:T(1024)S(1)} %get-tuple-element.13, s32[24000]{0:T(1024)S(1)} %get-tuple-element.12, s32[]{:T(128)} %constant.74.clone.1), kind=kCustom, calls=%fused_computation.50 | custom fusion | bytes 17284 | tf_op jit(solution)/shard_map/scatter | solution.py:29
  256.4 0.1 broadcast_in_dim.53
  256.5 3.1 reduce_max.24
  259.6 0.0 all-gather.2.cloned.1.call-done
  259.6 12.6 %fusion.25 = (f32[2,256]{1,0:T(2,128)S(1)}, f32[2,256,1500]{1,2,0:T(8,128)S(1)}) fusion(bf16[2,256,5120]{1,2,0:T(8,128)(2,1)} %all-gather.2.cloned.1.call-done, bf16[5120,1500]{0,1:T(8,128)(2,1)} %param.5), kind=kOutput, calls=%fused_computation.61 | convolution fusion | flops 7865087488 | bytes 23676928 | tf_op jit(solution)/shard_map/std,dv->stv/dot_general | solution.py:32
  272.3 0.0 copy-start
  272.3 35.5 %all-reduce.3 = (f32[2,256]{1,0:T(2,128)S(1)}, f32[256]{0:T(256)S(1)}) all-reduce(f32[2,256]{1,0:T(2,128)S(1)} %get-tuple-element.14, bf16[256]{0:T(256)(128)(2,1)S(1)} %reduce_max.24), channel_id=1, replica_groups=mesh['dp'=8,'tensor'=16] {'tensor'}, use_global_device_ids=true, to_apply=%region_1.2 | all-reduce | flops 768 | bytes 5632 | tf_op jit(solution)/shard_map/pmax | solution.py:36
  307.8 3.4 fusion.4
  311.3 28.7 %psum.22 = f32[256]{0:T(256)S(1)} all-reduce(f32[256]{0:T(256)S(1)} %fusion.4), channel_id=1, replica_groups=mesh['dp'=8,'tensor'=16] {'tensor'}, use_global_device_ids=true, to_apply=%region_11.12 | all-reduce | flops 256 | bytes 2048 | tf_op jit(solution)/shard_map/psum | solution.py:37
  340.0 4.9 divide_convert_fusion
  344.8 13.9 %gather_fusion = bf16[4320,256]{1,0:T(8,128)(2,1)} fusion(bf16[256,9496]{0,1:T(8,128)(2,1)} %divide_convert_fusion, s32[5120]{0:T(1024)S(1)} %pad_clamp_fusion), kind=kCustom, calls=%fused_computation | custom fusion | bytes 4440960 | tf_op jit(solution)/shard_map/jit(_take)/gather | solution.py:45
  358.7 4.1 gather.13
  362.8 3.0 broadcast_select_fusion
  365.8 4.4 all-to-all-start
  370.2 0.0 reduce-scatter.3.cloned.1.call-start
  370.4 0.0 copy-done
  370.4 0.4 fusion.6
  370.8 20.2 %all-to-all-done = bf16[256,16,270]{0,2,1:T(8,128)(2,1)} async-done(((bf16[256,16,270]{0,2,1:T(8,128)(2,1)}), bf16[256,16,270]{0,2,1:T(8,128)(2,1)}, u32[]{:S(2)}, u32[]{:S(2)}) %all-to-all-start) | async-done | bytes 2211872 | tf_op jit(solution)/shard_map/all_to_all | solution.py:46
  391.0 2.6 all_to_all.7
  393.7 5.0 gather_fusion.1
  398.6 0.3 convert_reduce_fusion
  398.9 28.8 %all-reduce.2 = (f32[2,256]{1,0:T(2,128)S(1)}, f32[256]{0:T(256)S(1)}) all-reduce(f32[2,256]{1,0:T(2,128)S(1)} %fusion.6, f32[256]{0:T(256)S(1)} %get-tuple-element.6), channel_id=1, replica_groups=mesh['dp'=8,'tensor'=16] {'tensor'}, use_global_device_ids=true, to_apply=%region_3.4 | all-reduce | flops 768 | bytes 6144 | tf_op jit(solution)/shard_map/psum | solution.py:37
  427.8 2.3 fusion.5
  430.1 0.1 slice.26
  430.1 0.4 fusion.14
  430.5 0.3 slice.37
  430.8 0.1 pad_maximum_fusion.3
  430.9 0.3 fusion.15
  431.2 14.0 %fusion = f32[2,256,5120]{1,2,0:T(8,128)} fusion(bf16[5120,1500]{0,1:T(8,128)(2,1)} %param.5, bf16[1,256,1500]{1,2,0:T(8,128)(2,1)S(1)} %fusion.15, bf16[1,256,1500]{1,2,0:T(8,128)(2,1)S(1)} %fusion.14), kind=kOutput, calls=%fused_computation.4 | convolution fusion | flops 7865088000 | bytes 27381760 | tf_op jit(solution)/shard_map/stv,dv->std/dot_general | solution.py:64
  445.2 0.0 reduce-scatter.3.cloned.1.call-update
  445.3 0.0 reduce-scatter.5.cloned.1.call-start
  445.3 16.1 %convolution_bitcast_fusion = f32[5120,1500]{0,1:T(8,128)} fusion(bf16[2,256,5120]{1,2,0:T(8,128)(2,1)} %all-gather.2.cloned.1.call-done, bf16[1,256,1500]{1,2,0:T(8,128)(2,1)S(1)} %fusion.15, bf16[1,256,1500]{1,2,0:T(8,128)(2,1)S(1)} %fusion.14), kind=kOutput, calls=%fused_computation.3 | convolution fusion | flops 7865088000 | bytes 37498880 | tf_op jit(solution)/shard_map/stc,stv->cv/dot_general | solution.py:69
  461.4 0.0 reduce-scatter.5.cloned.1.call-update
  461.4 93.1 %reduce-scatter.3.cloned.1.call-done = f32[2,256,320]{1,2,0:T(8,128)} async-done(((f32[2,256,5120]{1,2,0:T(8,128)}), f32[2,256,320]{1,2,0:T(8,128)}) %reduce-scatter.3.cloned.1.call-update) | async-done | bytes 655376 | tf_op jit(solution)/shard_map/reduce_scatter | solution.py:65
  554.5 1.8 convert_element_type.41
  556.4 158.5 %reduce-scatter.5.cloned.1.call-done = f32[640,1500]{0,1:T(8,128)} async-done(((f32[5120,1500]{0,1:T(8,128)}), f32[640,1500]{0,1:T(8,128)}) %reduce-scatter.5.cloned.1.call-update) | async-done | bytes 3840016 | tf_op jit(solution)/shard_map/reduce_scatter | solution.py:68
  (9 shorter events, 0.1 us)
Async XLA Ops:
  7.2 252.5 %all-gather.2.cloned.1.call-start = ((), (), s32[]{:S(2)}) async-start(), calls=%async_computation.3 | async-start | bytes 5570560 | tf_op jit(solution)/shard_map/all_gather | solution.py:31
  143.3 2.3 copy-start.1
  272.3 98.1 %copy-start = (f32[2,256,1500]{1,2,0:T(8,128)}, f32[2,256,1500]{1,2,0:T(8,128)S(1)}, u32[]{:S(2)}) copy-start(f32[2,256,1500]{1,2,0:T(8,128)S(1)} %get-tuple-element.15) | copy-start | bytes 9216004
  365.8 25.3 %all-to-all-start = ((bf16[256,16,270]{0,2,1:T(8,128)(2,1)}), bf16[256,16,270]{0,2,1:T(8,128)(2,1)}, u32[]{:S(2)}, u32[]{:S(2)}) async-start(bf16[256,16,270]{0,2,1:T(8,128)(2,1)} %broadcast_select_fusion), calls=%async_computation | async-start | bytes 4456448 | tf_op jit(solution)/shard_map/all_to_all | solution.py:46
  370.2 184.3 %reduce-scatter.3.cloned.1.call-start = ((), (), s32[]{:S(2)}) async-start(), calls=%async_computation.4 | async-start | bytes 11141120 | tf_op jit(solution)/shard_map/reduce_scatter | solution.py:65
  445.3 269.6 %reduce-scatter.5.cloned.1.call-start = ((), (), s32[]{:S(2)}) async-start(), calls=%async_computation.5 | async-start | bytes 34652160 | tf_op jit(solution)/shard_map/reduce_scatter | solution.py:68
Sparse Core Ops, SparseCore 0:
  10.1 59.7 all-gather.1
  445.4 109.1 reduce-scatter.2
  557.6 157.2 reduce-scatter.4
where the time goes:
time: 730 us; the launch traced here: 721 us
  waiting for transfers between devices  273 us (37%)
  other arithmetic  149 us (20%)
  local copies, waits for them, and re-layouts  145 us (20%)
  blocking collectives  93.1 us (13%)
  matrix products  42.8 us (6%)
  between operations  14 us (2%)
    reduce_scatter x1, waiting for transfers between devices, per_device(): lax.psum_scatter(jnp.einsum('stc,stv->cv', h_full, slopes, preferred_elem...  159 us
    another operation x4, other arithmetic  128 us
    scatter x1, local copies, waits for them, and re-layouts, per_device(): table = jnp.zeros((parts * bound,), jnp.int32).at[placing.reshape(-1)].se...  111 us
    reduce_scatter x1, waiting for transfers between devices, per_device(): lax.psum_scatter(terms, 'tensor', scatter_dimension=2, tiled=True)  93.1 us
    psum x2, blocking collectives, per_device(): lax.psum((jnp.sum(jnp.exp(logits - tpeak[:, None]), axis=1), jnp.sum(jnp....  57.5 us
    pmax x1, blocking collectives, per_device(): tpeak, dpeak = lax.pmax((tpeak_local, dpeak_local), 'tensor')  35.5 us
    all_to_all x1, waiting for transfers between devices, per_device(): lax.all_to_all(outgoing, 'tensor', split_axis=1, concat_axis=1, tiled=True)  20.2 us
    gather x2, local copies, waits for them, and re-layouts, per_device(): outgoing = jnp.take(owned_probs, table, axis=1)  17.9 us
  transfers between devices with their start and end apart: 4, of which 3 were waited for; matrix products, arithmetic and copies ran while one was open for 37% of the time, Pallas kernels for 0%

commit v1 on v0

v1 whole, which is shorter than its diff:
```python
import functools

import jax
import jax.numpy as jnp
from jax import lax
from jax.experimental import pallas as pl
from jax.experimental.pallas import tpu as pltpu
from jax.sharding import PartitionSpec as P

LOSS_SCALE = 256.0
STEP_DECAY = 0.8
MESH = pl.DeviceIdType.MESH
F32 = jnp.float32
BF16 = jnp.bfloat16
RING = 4
CORES = 2
LOW = -3.0e38


def ceil_to(value, unit):
    return (value + unit - 1) // unit * unit


def pick_kernel(slots, ids_ref, logits_ref, out_ref, stat_ref, place_ref, flipped, marks, tables):
    parts, block = ids_ref.shape
    tokens, shard = logits_ref.shape
    depth = flipped.shape[0]
    wide = ceil_to(block, 256)
    me = lax.axis_index("tensor")

    whole = shard // 256

    def flip(c, _):
        at = pl.multiple_of(c * 256, 256)
        flipped[pl.ds(at, 256), :] = logits_ref[:, pl.ds(at, 256)].T
        return 0

    lax.fori_loop(0, whole, flip, 0)
    rest = shard - whole * 256
    if rest:
        tail = jnp.concatenate(
            [logits_ref[:, whole * 256 :], jnp.full((tokens, 256 - rest), LOW, BF16)], axis=1
        )
        flipped[whole * 256 :, :] = tail.T

    rows = 256

    def peak_step(c, best):
        at = pl.multiple_of(c * rows, rows)
        part = flipped[pl.ds(at, rows), :].astype(F32).reshape(rows // 8, 8, tokens)
        return jnp.maximum(best, jnp.max(part, axis=0))

    best = lax.fori_loop(0, depth // rows, peak_step, jnp.full((8, tokens), LOW, F32))
    peak = jnp.max(best, axis=0, keepdims=True)

    def sum_step(c, acc):
        at = pl.multiple_of(c * rows, rows)
        part = jnp.exp(flipped[pl.ds(at, rows), :].astype(F32) - peak).reshape(rows // 8, 8, tokens)
        return acc + jnp.sum(part, axis=0)

    acc = lax.fori_loop(0, depth // rows, sum_step, jnp.zeros((8, tokens), F32))
    total = jnp.sum(acc, axis=0, keepdims=True)
    row = lax.broadcasted_iota(jnp.int32, (8, tokens), 0)
    stat_ref[...] = jnp.where(row == 0, peak, jnp.where(row == 1, total, 0.0))

    ids = jnp.concatenate([ids_ref[...], jnp.full((parts, wide - block), -1, jnp.int32)], axis=1)
    local = ids - me * shard
    mine = (local >= 0) & (local < shard)
    own = jnp.concatenate(
        [ids_ref[pl.ds(me, 1), :], jnp.full((1, wide - block), -1, jnp.int32)], axis=1
    )
    start = lax.broadcasted_iota(jnp.int32, (parts, wide), 0) * shard
    from_owner = (own >= start) & (own < start + shard)
    hits = jnp.concatenate([jnp.where(mine, 1.0, 0.0), jnp.where(from_owner, 1.0, 0.0)], axis=0)
    before = lax.broadcasted_iota(jnp.int32, (wide, wide), 0)
    after = lax.broadcasted_iota(jnp.int32, (wide, wide), 1)
    upper = jnp.where(before <= after, 1.0, 0.0).astype(BF16)
    ranks = jnp.dot(hits.astype(BF16), upper, preferred_element_type=F32) - 1.0
    owner = lax.broadcasted_iota(jnp.int32, (parts, wide), 0).astype(F32) * float(slots)
    place = jnp.sum(jnp.where(from_owner, owner + ranks[parts:], 0.0), axis=0, keepdims=True)
    place = jnp.where(own >= 0, place, -1.0)
    place_ref[...] = jnp.broadcast_to(place, (8, wide)).astype(jnp.int32)
    tables[0] = jnp.where(mine, ranks[:parts], -1.0)
    tables[1] = jnp.where(mine, local >> 8, 0).astype(F32)
    tables[2] = jnp.where(mine, local & 255, 0).astype(F32)

    def block_step(b, _):
        rank = tables[0, pl.ds(b, 1), :]
        high = jnp.broadcast_to(tables[1, pl.ds(b, 1), :], (128, wide)).astype(BF16)
        low = jnp.broadcast_to(tables[2, pl.ds(b, 1), :] , (128, wide)).astype(BF16)
        slot = lax.broadcasted_iota(jnp.int32, (slots, wide), 0).astype(F32)
        hot = jnp.where(slot == rank, 1.0, 0.0).astype(BF16)
        nt = (((1,), (1,)), ((), ()))
        used = lax.dot_general(hot, jnp.ones((128, wide), BF16), nt, preferred_element_type=F32)
        high_of = lax.dot_general(hot, high, nt, preferred_element_type=F32)
        low_of = lax.dot_general(hot, low, nt, preferred_element_type=F32)
        high_of = jnp.where(used > 0.5, high_of, -1.0)
        lane = lax.broadcasted_iota(jnp.int32, (slots, 128), 1).astype(F32)
        left = jnp.where(low_of == lane, 1.0, 0.0).astype(BF16)
        right = jnp.where(low_of == lane + 128.0, 1.0, 0.0).astype(BF16)
        high_of = high_of.astype(BF16)
        zero = jnp.zeros((slots, 128), BF16)
        for c in range(depth // 256):
            here = high_of == jnp.asarray(float(c), BF16)
            marks[:, c * 256 : c * 256 + 128] = jnp.where(here, left, zero)
            marks[:, c * 256 + 128 : c * 256 + 256] = jnp.where(here, right, zero)
        out_ref[b] = jnp.dot(marks[...], flipped[...], preferred_element_type=F32).astype(BF16)
        return 0

    lax.fori_loop(0, parts, block_step, 0)


def pick(ids, logits, slots):
    parts, block = ids.shape
    tokens, shard = logits.shape
    depth = ceil_to(shard, 256)
    wide = ceil_to(block, 256)
    vmem = pl.BlockSpec(memory_space=pltpu.VMEM)
    return pl.pallas_call(
        functools.partial(pick_kernel, slots),
        out_shape=(
            jax.ShapeDtypeStruct((parts, slots, tokens), BF16),
            jax.ShapeDtypeStruct((8, tokens), F32),
            jax.ShapeDtypeStruct((8, wide), jnp.int32),
        ),
        in_specs=[vmem, vmem],
        out_specs=(vmem, vmem, vmem),
        scratch_shapes=[
            pltpu.VMEM((depth, tokens), BF16),
            pltpu.VMEM((slots, depth), BF16),
            pltpu.VMEM((3, parts, wide), F32),
        ],
        compiler_params=pltpu.CompilerParams(vmem_limit_bytes=50 * 2**20),
        cost_estimate=pl.CostEstimate(
            flops=2 * parts * slots * depth * tokens, bytes_accessed=4 * tokens * shard, transcendentals=tokens * shard
        ),
        name="pick",
    )(ids, logits)


def as_column(rows):
    wide = jnp.broadcast_to(rows[0:1, :], (128, rows.shape[1]))
    return wide.T[:, 0:1]


def as_row(column):
    wide = jnp.broadcast_to(column, (column.shape[0], 128))
    return wide.T[0:1, :]


def tail_kernel(
    sizes,
    scores_ref,
    inc_ref,
    stat_ref,
    place_ref,
    ht_ref,
    w_ref,
    gh_ref,
    gw_ref,
    probs,
    slopes,
    h_peer,
    w_buf,
    terms,
    exch,
    x_out,
    x_far,
    x_in,
    p_out,
    p_far,
    p_in,
    q_out,
    q_far,
    q_in,
    p2_out,
    p2_far,
    p2_in,
    q2_out,
    q2_far,
    q2_in,
    ex_send,
    ex_recv,
    pair_send,
    pair_recv,
    w_sem,
    ring_send,
    ring_recv,
):
    steps, tokens, block, wide = sizes
    parts = RING * RING
    both = steps * tokens
    dp = lax.axis_index("dp")
    tensor = lax.axis_index("tensor")
    x, core = dp // CORES, dp % CORES
    z, y = tensor // RING, tensor % RING
    d = ht_ref.shape[0]
    sub = d // parts
    own_rows = d // (RING * CORES)
    half = own_rows // 2

    def x_peer(by):
        return (((x + by) % RING) * CORES + core, tensor)

    def z_peer(by):
        return (dp, ((z + by) % RING) * RING + y)

    def y_peer(by):
        return (dp, z * RING + (y + by) % RING)

    partner = (x * CORES + 1 - core, tensor)

    barrier = pltpu.get_barrier_semaphore()
    for i in range(1, parts):
        pl.semaphore_signal(barrier, inc=1, device_id=(dp, (tensor + i) % parts), device_id_type=MESH)
    pl.semaphore_signal(barrier, inc=1, device_id=partner, device_id_type=MESH)
    for by in (1, RING - 1):
        pl.semaphore_signal(barrier, inc=1, device_id=x_peer(by), device_id_type=MESH)
    pl.semaphore_wait(barrier, parts + 2)

    def remote(src, dst, send, recv, device):
        return pltpu.make_async_remote_copy(
            src_ref=src, dst_ref=dst, send_sem=send, recv_sem=recv, device_id=device, device_id_type=MESH
        )

    def exchange(turn):
        copies = []
        for i in range(1, parts):
            copies.append(
                remote(
                    exch.at[turn, tensor],
                    exch.at[turn, tensor],
                    ex_send.at[turn, i],
                    ex_recv.at[turn, i],
                    (dp, (tensor + i) % parts),
                )
            )
        for copy in copies:
            copy.start()
        return copies

    exch[0, tensor, :, 0:tokens] = stat_ref[...]
    exch[0, tensor, :, tokens:both] = stat_ref[...]
    first = exchange(0)

    pair = []
    for i in range(RING):
        rows = pl.multiple_of((i * CORES + 1 - core) * own_rows, own_rows)
        pair.append(
            remote(ht_ref.at[pl.ds(rows, own_rows)], h_peer.at[i], pair_send.at[i], pair_recv.at[i], partner)
        )
        pair[-1].start()

    w_rows = w_buf.shape[1]

    def w_copy(i, slot):
        rows = pl.multiple_of(i * w_rows, w_rows)
        return pltpu.make_async_copy(w_ref.at[pl.ds(rows, w_rows)], w_buf.at[slot], w_sem.at[slot])

    w_copy(0, 0).start()
    w_copy(1, 1).start()

    band = 64
    lanes = lax.broadcasted_iota(jnp.int32, (band, block), 1)

    top = jnp.concatenate([jnp.max(scores_ref[pl.ds(i, 128), :], axis=1, keepdims=True) for i in range(0, both, 128)], axis=0)
    mass_sum = jnp.concatenate(
        [
            jnp.sum(jnp.exp(scores_ref[pl.ds(i, 128), :] - top[i : i + 128]), axis=1, keepdims=True)
            for i in range(0, both, 128)
        ],
        axis=0,
    )
    top_row = as_row(top)
    sum_row = as_row(mass_sum)

    slots_all = inc_ref.shape[0]
    place = place_ref[0:1, :]
    n_tile = 512
    for n in range(0, wide, n_tile):
        place_n = place[:, n : n + n_tile]
        row = lax.broadcasted_iota(jnp.int32, (256, n_tile), 0)

        def pick_step(c, acc):
            at = pl.multiple_of(c * 256, 256)
            hot = jnp.where(row + at == place_n, 1.0, 0.0).astype(BF16)
            return acc + lax.dot_general(
                inc_ref[pl.ds(at, 256), :], hot, (((0,), (0,)), ((), ())), preferred_element_type=F32
            )

        probs[:, n : n + n_tile] = lax.fori_loop(
            0, slots_all // 256, pick_step, jnp.zeros((tokens, n_tile), F32)
        )

    for copy in first:
        copy.wait()
    peaks = [exch[0, i, 0:1, :] for i in range(parts)]
    t_peak = functools.reduce(jnp.maximum, peaks)
    t_total = sum(exch[0, i, 1:2, :] * jnp.exp(peaks[i] - t_peak) for i in range(parts))
    t_peak_c = as_column(t_peak[:, 0:tokens])
    t_total_c = as_column(t_total[:, 0:tokens])
    masses = []
    for i in range(0, tokens, band):
        value = jnp.exp(probs[i : i + band, :] - t_peak_c[i : i + band]) / t_total_c[i : i + band]
        inside = lax.broadcasted_iota(jnp.int32, (band, wide), 1) < block
        value = jnp.where(inside, value, 0.0).astype(BF16).astype(F32)
        probs[i : i + band, :] = value
        masses.append(jnp.sum(value, axis=1, keepdims=True))
    mass_row = as_row(jnp.concatenate(masses, axis=0))

    kind = lax.broadcasted_iota(jnp.int32, (8, both), 0)
    mass_row = jnp.concatenate([mass_row] * steps, axis=1)
    exch[1, tensor] = jnp.where(
        kind == 0, top_row, jnp.where(kind == 1, sum_row, jnp.where(kind == 2, mass_row, 0.0))
    )
    second = exchange(1)
    for copy in second:
        copy.wait()
    tops = [exch[1, i, 0:1, :] for i in range(parts)]
    top_all = functools.reduce(jnp.maximum, tops)
    sum_all = sum(exch[1, i, 1:2, :] * jnp.exp(tops[i] - top_all) for i in range(parts))
    mass_all = sum(exch[1, i, 2:3, :] for i in range(parts))
    top_c = as_column(top_all)
    sum_c = as_column(sum_all)
    mass_c = as_column(mass_all[:, 0:tokens])

    for step in range(steps):
        for i in range(0, tokens, band):
            r = step * tokens + i
            soft = jnp.exp(scores_ref[r : r + band, :] - top_c[r : r + band]) / sum_c[r : r + band]
            if step == 0:
                shifted = probs[i : i + band, 0:block]
                mass = mass_c[i : i + band]
            else:
                got = min(band, tokens - i - step)
                shifted = probs[i + step : i + step + got, 0:block]
                mass = mass_c[i + step : i + step + got]
                if got < band:
                    shifted = jnp.concatenate([shifted, jnp.zeros((band - got, block), F32)], axis=0)
                    mass = jnp.concatenate([mass, jnp.zeros((band - got, 1), F32)], axis=0)
            slope = LOSS_SCALE * STEP_DECAY**step * (soft * mass - shifted)
            slope = jnp.concatenate([slope, jnp.zeros((band, wide - block), F32)], axis=1)
            slopes[0, r : r + band, :] = slope.astype(BF16)

    swap = remote(slopes.at[0], slopes.at[1], pair_send.at[RING], pair_recv.at[RING], partner)
    swap.start()
    for copy in pair:
        copy.wait()
    swap.wait()

    piece = 160

    def head_part(by, rows):
        chip = (x + by) % RING
        at = pl.multiple_of((chip * CORES + core) * own_rows + rows, piece)
        mine = jnp.dot(ht_ref[pl.ds(at, piece), :], slopes[0], preferred_element_type=F32)
        return mine + jnp.dot(
            h_peer[chip, pl.ds(pl.multiple_of(rows, piece), piece), :], slopes[1], preferred_element_type=F32
        )

    def link(n, src, dst, device):
        return remote(src, dst, ring_send.at[n], ring_recv.at[n], device)

    count = half // piece

    def fill(out, by, first_row, rows):
        def go(i, _):
            at = pl.multiple_of(rows + i * piece, piece)
            to = pl.multiple_of(first_row + i * piece, piece)
            out[pl.ds(to, piece), :] = head_part(by, at).astype(BF16)
            return 0

        lax.fori_loop(0, count, go, 0)

    fill(x_out.at[0], 2, 0, 0)
    far_r = link(0, x_out.at[0], x_far.at[0], x_peer(1))
    far_r.start()
    fill(x_out.at[1], 2, 0, half)
    far_l = link(1, x_out.at[1], x_far.at[1], x_peer(RING - 1))
    far_l.start()
    fill(x_out.at[3], 1, 0, half)
    free_r = link(2, x_out.at[3], x_in.at[1], x_peer(1))
    free_r.start()
    fill(x_out.at[4], RING - 1, 0, 0)
    free_l = link(3, x_out.at[4], x_in.at[2], x_peer(RING - 1))
    free_l.start()

    per = w_rows // sub

    def term_step(i, _):
        slot = i % 2
        w_copy(i, slot).wait()
        for s in range(per):
            terms[i * per + s] = lax.dot_general(
                w_buf[slot, s * sub : (s + 1) * sub, :],
                slopes[0, :, 0:block],
                (((1,), (1,)), ((), ())),
                preferred_element_type=F32,
            )

        @pl.when(i + 2 < d // w_rows)
        def _():
            w_copy(i + 2, slot).start()

        return 0

    lax.fori_loop(0, d // w_rows, term_step, 0)

    pair_of = RING // 2
    p_at, q_at = pl.ds(0, tokens), pl.ds(tokens, tokens)

    def p_term(by, n):
        return terms[((z + by) % RING) * RING + n, :, p_at]

    def q_term(by, n):
        return terms[n * RING + (y + by) % RING, :, q_at]

    def start_first(term, out, far, into, peer, base):
        def put(slot, by, first, extra=None):
            for n in range(pair_of):
                value = term(by, first + n)
                if extra is not None:
                    value = value + extra[n].astype(F32)
                out[slot, n] = value.astype(BF16)

        put(0, 2, 0)
        a = link(base, out.at[0], far.at[0], peer(1))
        a.start()
        put(1, 2, pair_of)
        b = link(base + 1, out.at[1], far.at[1], peer(RING - 1))
        b.start()
        put(3, 1, pair_of)
        c = link(base + 2, out.at[3], into.at[1], peer(1))
        c.start()
        put(4, RING - 1, 0)
        e = link(base + 3, out.at[4], into.at[2], peer(RING - 1))
        e.start()

        def later():
            a.wait()
            put(2, 1, 0, far.at[0])
            f = link(base + 4, out.at[2], into.at[0], peer(1))
            f.start()
            b.wait()
            put(5, RING - 1, pair_of, far.at[1])
            g = link(base + 5, out.at[5], into.at[3], peer(RING - 1))
            g.start()

            def done():
                for copy in (c, e, f, g):
                    copy.wait()

            return done

        return later

    p_later = start_first(p_term, p_out, p_far, p_in, z_peer, 6)
    q_later = start_first(q_term, q_out, q_far, q_in, y_peer, 12)
    p_done = p_later()
    q_done = q_later()

    far_r.wait()

    def add_right(i, _):
        at = pl.multiple_of(i * piece, piece)
        value = head_part(1, at) + x_far[0, pl.ds(at, piece), :].astype(F32)
        x_out[2, pl.ds(at, piece), :] = value.astype(BF16)
        return 0

    lax.fori_loop(0, count, add_right, 0)
    dep_r = link(4, x_out.at[2], x_in.at[0], x_peer(1))
    dep_r.start()
    far_l.wait()

    def add_left(i, _):
        at = pl.multiple_of(i * piece, piece)
        value = head_part(RING - 1, half + at) + x_far[1, pl.ds(at, piece), :].astype(F32)
        x_out[5, pl.ds(at, piece), :] = value.astype(BF16)
        return 0

    lax.fori_loop(0, count, add_left, 0)
    dep_l = link(5, x_out.at[5], x_in.at[3], x_peer(RING - 1))
    dep_l.start()

    p_done()
    for n in range(RING):
        got = p_in[n // pair_of, n % pair_of].astype(F32) + p_in[2 + n // pair_of, n % pair_of].astype(F32)
        mine = z * RING + n
        terms[mine, :, p_at] = terms[mine, :, p_at] + got
    q_done()
    for n in range(RING):
        got = q_in[n // pair_of, n % pair_of].astype(F32) + q_in[2 + n // pair_of, n % pair_of].astype(F32)
        mine = n * RING + y
        terms[mine, :, q_at] = terms[mine, :, q_at] + got

    cut = sub // 2

    def start_second(lane, index, out, far, into, peer, base):
        def put(slot, by, first, extra=None):
            value = terms[index(by), first : first + cut, lane]
            if extra is not None:
                value = value + extra[...].astype(F32)
            out[slot] = value.astype(BF16)

        put(0, 2, 0)
        a = link(base, out.at[0], far.at[0], peer(1))
        a.start()
        put(1, 2, cut)
        b = link(base + 1, out.at[1], far.at[1], peer(RING - 1))
        b.start()
        put(3, 1, cut)
        c = link(base + 2, out.at[3], into.at[1], peer(1))
        c.start()
        put(4, RING - 1, 0)
        e = link(base + 3, out.at[4], into.at[2], peer(RING - 1))
        e.start()

        def later():
            a.wait()
            put(2, 1, 0, far.at[0])
            f = link(base + 4, out.at[2], into.at[0], peer(1))
            f.start()
            b.wait()
            put(5, RING - 1, cut, far.at[1])
            g = link(base + 5, out.at[5], into.at[3], peer(RING - 1))
            g.start()

            def done():
                for copy in (c, e, f, g):
                    copy.wait()
                for n in range(2):
                    value = terms[tensor, n * cut : (n + 1) * cut, lane]
                    value = value + into[n].astype(F32) + into[2 + n].astype(F32)
                    gh_ref[n * cut : (n + 1) * cut, lane] = value.astype(BF16)

            return done

        return later

    p2_later = start_second(p_at, lambda by: z * RING + (y + by) % RING, p2_out, p2_far, p2_in, y_peer, 18)
    q2_later = start_second(q_at, lambda by: ((z + by) % RING) * RING + y, q2_out, q2_far, q2_in, z_peer, 24)
    p2_done = p2_later()
    q2_done = q2_later()

    def own_step(i, _):
        at = pl.multiple_of(i * piece, piece)
        gw_ref[pl.ds(at, piece), :] = head_part(0, at)[:, 0:block]
        return 0

    lax.fori_loop(0, own_rows // piece, own_step, 0)
    p2_done()
    q2_done()

    for copy in (free_r, free_l, dep_r, dep_l):
        copy.wait()
    for h in range(2):

        def last_step(i, _, h=h):
            at = pl.multiple_of(i * 32, 32)
            to = pl.multiple_of(h * half + i * 32, 32)
            got = x_in[h, pl.ds(at, 32), :].astype(F32) + x_in[2 + h, pl.ds(at, 32), :].astype(F32)
            gw_ref[pl.ds(to, 32), :] = gw_ref[pl.ds(to, 32), :] + got[:, 0:block]
            return 0

        lax.fori_loop(0, half // 32, last_step, 0)


def tail(scores, incoming, stat, place, ht, w, tokens):
    both, block = scores.shape
    steps = both // tokens
    d = ht.shape[0]
    parts = RING * RING
    sub = d // parts
    own_rows = d // (RING * CORES)
    half = own_rows // 2
    wide = ceil_to(block, 256)
    vmem = pl.BlockSpec(memory_space=pltpu.VMEM)
    ring_x = [(6, half, wide), (2, half, wide), (4, half, wide)]
    ring_1 = [(6, 2, sub, tokens), (2, 2, sub, tokens), (4, 2, sub, tokens)]
    ring_2 = [(6, sub // 2, tokens), (2, sub // 2, tokens), (4, sub // 2, tokens)]
    return pl.pallas_call(
        functools.partial(tail_kernel, (steps, tokens, block, wide)),
        out_shape=(
            jax.ShapeDtypeStruct((sub, both), BF16),
            jax.ShapeDtypeStruct((own_rows, block), F32),
        ),
        in_specs=[vmem, vmem, vmem, vmem, vmem, pl.BlockSpec(memory_space=pl.ANY)],
        out_specs=(vmem, vmem),
        scratch_shapes=[
            pltpu.VMEM((tokens, wide), F32),
            pltpu.VMEM((2, both, wide), BF16),
            pltpu.VMEM((RING, own_rows, both), BF16),
            pltpu.VMEM((2, 2 * sub, block), BF16),
            pltpu.VMEM((parts, sub, both), F32),
            pltpu.VMEM((2, parts, 8, both), F32),
        ]
        + [pltpu.VMEM(shape, BF16) for shape in ring_x + ring_1 + ring_1 + ring_2 + ring_2]
        + [
            pltpu.SemaphoreType.DMA((2, parts)),
            pltpu.SemaphoreType.DMA((2, parts)),
            pltpu.SemaphoreType.DMA((RING + 1,)),
            pltpu.SemaphoreType.DMA((RING + 1,)),
            pltpu.SemaphoreType.DMA((2,)),
            pltpu.SemaphoreType.DMA((30,)),
            pltpu.SemaphoreType.DMA((30,)),
        ],
        compiler_params=pltpu.CompilerParams(
            collective_id=3, has_side_effects=True, vmem_limit_bytes=63 * 2**20
        ),
        name="tail",
    )(scores, incoming, stat, place, ht, w)


def per_device(hidden, draft_head, target_logits, draft_to_target):
    parts = lax.axis_size("tensor")
    steps, tokens, width = hidden.shape
    block = draft_to_target.shape[0] // parts
    heavy = block // 8
    bound = heavy + (block - heavy + parts - 1) // parts
    slots = ceil_to(bound, 16)

    flat = hidden.reshape(steps * tokens, width).T
    ht = lax.all_gather(flat, "tensor", axis=0, tiled=True)
    picked, stat, place = pick(draft_to_target.reshape(parts, block), target_logits, slots)
    incoming = lax.all_to_all(picked, "tensor", split_axis=0, concat_axis=0, tiled=True)
    scores = lax.dot_general(ht, draft_head, (((0,), (0,)), ((), ())), preferred_element_type=F32)
    gh, gw = tail(scores, incoming.reshape(parts * slots, tokens), stat, place, ht, draft_head, tokens)
    return gh.T.reshape(steps, tokens, width), gw


def solution(mesh):
    in_specs = (P(None, "dp", "tensor"), P(None, "tensor"), P("dp", "tensor"), P())
    out_specs = (P(None, "dp", "tensor"), P("dp", "tensor"))
    return jax.shard_map(
        per_device, mesh=mesh, in_specs=in_specs, out_specs=out_specs, check_vma=False
    )
```

time: 730 us -> 257 us (0.35)
  waiting for transfers between devices: 273 us -> 0.02 us
  Pallas kernels: 0 us -> 179 us
  other arithmetic: 149 us -> 0 us
  local copies, waits for them, and re-layouts: 145 us -> 39.2 us
  blocking collectives: 93.1 us -> 0 us
  matrix products: 42.8 us -> 14.4 us
    reduce_scatter x2 -> x0, waiting for transfers between devices: 252 us -> none  [the longest x1 159 us: per_device(): lax.psum_scatter(jnp.einsum('stc,stv->cv', h_full, slopes, preferred_elem...]
    pallas_call x0 -> x2, Pallas kernels: none -> 179 us  [the longest x1 108 us: tail(): pl.pallas_call(functools.partial(tail_kernel, (steps, tokens, block, wide...]
    another operation x5 -> x0, other arithmetic: 128 us -> none
    scatter x1 -> x0, local copies, waits for them, and re-layouts: 111 us -> none  [per_device(): table = jnp.zeros((parts * bound,), jnp.int32).at[placing.reshape(-1)].se...]
    psum x2 -> x0, blocking collectives: 57.5 us -> none  [per_device(): lax.psum((jnp.sum(jnp.exp(logits - tpeak[:, None]), axis=1), jnp.sum(jnp....]
    pmax x1 -> x0, blocking collectives: 35.5 us -> none  [per_device(): tpeak, dpeak = lax.pmax((tpeak_local, dpeak_local), 'tensor')]
    unnamed x4 -> x7, local copies, waits for them, and re-layouts: 0.01 us -> 34.8 us
    dot_general x3 -> x1, matrix products: 42.8 us -> 14.4 us  [per_device(): lax.dot_general(ht, draft_head, (((0,), (0,)), ((), ())), preferred_eleme...]
  transfers between devices with their start and end apart: 4 -> 2, of which waited for: 3 -> 0; matrix products, arithmetic and copies ran while one was open for 37% -> 17% of each run, Pallas kernels for 0% -> 28%
where the time goes in v1:
time: 257 us; the launch traced here: 255 us
  Pallas kernels  179 us (70%)
  local copies, waits for them, and re-layouts  39.2 us (15%)
  matrix products  14.4 us (6%)
  between operations  14.1 us (5%)
  starting transfers between devices  8.7 us (3%)
    pallas_call x1, Pallas kernels, tail(): pl.pallas_call(functools.partial(tail_kernel, (steps, tokens, block, wide...  108 us
    pallas_call x1, Pallas kernels, pick(): pl.pallas_call(functools.partial(pick_kernel, slots), out_shape=(jax.Shap...  71.2 us
    unnamed x7, local copies, waits for them, and re-layouts  34.8 us
    dot_general x1, matrix products, per_device(): lax.dot_general(ht, draft_head, (((0,), (0,)), ((), ())), preferred_eleme...  14.4 us
    all_to_all x1, starting transfers between devices, per_device(): lax.all_to_all(picked, 'tensor', split_axis=0, concat_axis=0, tiled=True)  8.66 us
  transfers between devices with their start and end apart: 2, of which 0 were waited for; matrix products, arithmetic and copies ran while one was open for 17% of the time, Pallas kernels for 28%

profile of v1, /device:TPU:1, one launch (start us, length us, event | category | flops | bytes accessed | tf_op | source)
XLA Modules:
  0.0 255.4 jit_solution(8963989045756471719)
XLA Ops:
  7.2 0.0 all-gather.2.cloned.1.call-start
  7.2 1.7 copy.14
  8.9 0.0 all-gather.2.cloned.1.call-update
  9.0 1.0 reshape.17.ids_ref
  10.0 7.5 %copy.7.logits_ref = bf16[256,9496]{1,0:T(8,128)(2,1)} copy(bf16[256,9496]{0,1:T(8,128)(2,1)} %param.6) | data formatting | bytes 9723904 | tf_op args[2]
  17.5 71.2 %pick.1 = (bf16[16,272,256]{2,1,0:T(8,128)(2,1)}, f32[8,256]{1,0:T(8,128)S(1)}, s32[8,1536]{1,0:T(8,128)S(1)}) custom-call(s32[16,1500]{1,0:T(8,128)S(1)} %reshape.17.ids_ref, bf16[256,9496]{1,0:T(8,128)(2,1)} %copy.7.logits_ref), custom_call_target="tpu_custom_call" | custom-call | flops 21676163072 | bytes 9723904 | tf_op jit(solution)/shard_map/pick/pallas_call | solution.py:119
  88.7 0.0 copy-start
  88.7 0.6 copy-done
  89.3 0.0 copy-start.1
  89.3 0.6 copy-done.1
  89.9 8.7 %all-to-all-start = ((bf16[16,272,256]{2,1,0:T(8,128)(2,1)}), bf16[16,272,256]{2,1,0:T(8,128)(2,1)}, u32[]{:S(2)}, u32[]{:S(2)}) async-start(bf16[16,272,256]{2,1,0:T(8,128)(2,1)} %get-tuple-element.7), calls=%async_computation | async-start | bytes 4456448 | tf_op jit(solution)/shard_map/all_to_all | solution.py:625
  98.6 20.6 %copy.9.w_ref = bf16[5120,1500]{1,0:T(8,128)(2,1)} copy(bf16[5120,1500]{0,1:T(8,128)(2,1)} %param.5) | data formatting | bytes 30720000 | tf_op args[1]
  119.1 0.0 all-gather.2.cloned.1.call-done.ht_ref
  119.2 14.4 %fusion.scores_ref = f32[512,1500]{1,0:T(8,128)} fusion(bf16[5120,512]{1,0:T(8,128)(2,1)} %all-gather.2.cloned.1.call-done.ht_ref, bf16[5120,1500]{0,1:T(8,128)(2,1)} %param.5), kind=kOutput, calls=%fused_computation.1 | convolution fusion | flops 7864320000 | bytes 23674880 | tf_op jit(solution)/shard_map/dot_general | solution.py:626
  133.6 0.0 all-to-all-done
  133.6 107.8 %tail.1 = (bf16[320,512]{1,0:T(8,128)(2,1)}, f32[640,1500]{1,0:T(8,128)}) custom-call(f32[512,1500]{1,0:T(8,128)} %fusion.scores_ref, bf16[4352,256]{1,0:T(8,128)(2,1)} %bitcast.1.inc_ref, f32[8,256]{1,0:T(8,128)} %copy-done.1, s32[8,1536]{1,0:T(8,128)} %copy-done, bf16[5120,512]{1,0:T(8,128)(2,1)} %all-gather.2.cloned.1.call-done.ht_ref, ...), custom_call_target="tpu_custom_call" | custom-call | tf_op jit(solution)/shard_map/tail/pallas_call | solution.py:581
  241.4 1.7 copy.16
  243.1 5.4 %copy.11 = f32[640,1500]{0,1:T(8,128)} copy(f32[640,1500]{1,0:T(8,128)} %get-tuple-element.13) | data formatting | bytes 7680000
Async XLA Ops:
  7.2 112.0 %all-gather.2.cloned.1.call-start = ((), (), s32[]{:S(2)}) async-start(), calls=%async_computation.1 | async-start | bytes 5570560 | tf_op jit(solution)/shard_map/all_gather | solution.py:623
  88.7 0.6 copy-start
  89.3 0.6 copy-start.1
  89.9 43.7 %all-to-all-start = ((bf16[16,272,256]{2,1,0:T(8,128)(2,1)}), bf16[16,272,256]{2,1,0:T(8,128)(2,1)}, u32[]{:S(2)}, u32[]{:S(2)}) async-start(bf16[16,272,256]{2,1,0:T(8,128)(2,1)} %get-tuple-element.7), calls=%async_computation | async-start | bytes 4456448 | tf_op jit(solution)/shard_map/all_to_all | solution.py:625
Sparse Core Ops, SparseCore 0:
  10.7 59.7 all-gather.1

commit v2 on v0

v2 whole, which is shorter than its diff:
```python
import functools

import jax
import jax.numpy as jnp
from jax import lax
from jax.experimental import pallas as pl
from jax.experimental.pallas import tpu as pltpu
from jax.sharding import PartitionSpec as P

LOSS_SCALE = 256.0
STEP_DECAY = 0.8
MESH = pl.DeviceIdType.MESH
F32 = jnp.float32
BF16 = jnp.bfloat16
I32 = jnp.int32
RING = 4
CORES = 2
PARTS = RING * RING
LOW = -3.0e38
NT = (((1,), (1,)), ((), ()))


def ceil_to(value, unit):
    return (value + unit - 1) // unit * unit


def places():
    dp = lax.axis_index("dp")
    tensor = lax.axis_index("tensor")
    x, core = dp // CORES, dp % CORES
    z, y = tensor // RING, tensor % RING
    return dp, tensor, x, core, z, y


def remote(src, dst, send, recv, device):
    return pltpu.make_async_remote_copy(
        src_ref=src, dst_ref=dst, send_sem=send, recv_sem=recv, device_id=device, device_id_type=MESH
    )


def pieces_of(rows):
    half = rows // 2
    first = ceil_to(half // 2, 16)
    return [(0, first), (first, half - first), (half, first), (half + first, half - first)]


def front_kernel(
    sizes,
    hid_ref,
    ids_ref,
    logits_ref,
    w_ref,
    sl_ref,
    hn_ref,
    ht,
    h_peer,
    w_buf,
    source,
    picked,
    outgoing,
    incoming,
    expo,
    probs,
    rank_v,
    tab_v,
    place_v,
    ex1,
    ex2,
    tab_s,
    place_s,
    ag_send,
    ag_recv,
    a2a_send,
    a2a_recv,
    ex_send,
    ex_recv,
    pair_send,
    pair_recv,
    w_sem,
    s_sem,
):
    steps, tokens, block, rows, slots = sizes
    shard = logits_ref.shape[0]
    sub = hid_ref.shape[1]
    both = steps * tokens
    wide = ceil_to(block, 256)
    lane_parts = tokens // 128
    dp, tensor, x, core, z, y = places()
    partner = (x * CORES + 1 - core, tensor)

    def z_peer(by):
        return (dp, ((z + by) % RING) * RING + y)

    def y_peer(by):
        return (dp, z * RING + (y + by) % RING)

    def group_peer(i):
        return (dp, (tensor + i) % PARTS)

    chunk = w_buf.shape[2]

    def w_copy(i):
        return pltpu.make_async_copy(w_ref.at[:, pl.ds(i * chunk, chunk)], w_buf.at[i % 2], w_sem.at[i % 2])

    w_copy(0).start()
    w_copy(1).start()
    for s in range(steps):
        ht[s, z, y] = hid_ref[s]

    barrier = pltpu.get_barrier_semaphore()
    for i in range(1, PARTS):
        pl.semaphore_signal(barrier, inc=1, device_id=group_peer(i), device_id_type=MESH)
    pl.semaphore_signal(barrier, inc=1, device_id=partner, device_id_type=MESH)
    pl.semaphore_wait(barrier, PARTS)

    def gather_ring(half, at, peer, base):
        right, left = (at + 1) % RING, (at + RING - 1) % RING

        def copy(n, r, h, by):
            ref = half(r, h)
            return remote(ref, ref, ag_send.at[base + n], ag_recv.at[base + n], peer(by))

        r1 = copy(0, at, 0, 1)
        l1 = copy(1, at, 1, RING - 1)
        r2 = copy(2, at, 1, 1)
        l2 = copy(3, at, 0, RING - 1)
        for c in (r1, l1, r2, l2):
            c.start()

        def pass_on():
            r1.wait()
            r3 = copy(4, left, 0, 1)
            r3.start()
            l1.wait()
            l3 = copy(5, right, 1, RING - 1)
            l3.start()

            def finish():
                for c in (r2, l2, r3, l3):
                    c.wait()

            return finish

        return pass_on

    def half_rows(s, at_z, at_y, h):
        return ht.at[s, at_z, at_y, pl.ds(h * (sub // 2), sub // 2)]

    two = RING // 2
    p1 = gather_ring(lambda r, h: half_rows(0, z, r, h), y, y_peer, 0)
    q1 = gather_ring(lambda r, h: half_rows(1, r, y, h), z, z_peer, 6)

    ids = jnp.concatenate([ids_ref[...], jnp.full((PARTS, wide - block), -1, I32)], axis=1)
    local = ids - tensor * shard
    mine = (local >= 0) & (local < shard)
    own = jnp.sum(jnp.where(lax.broadcasted_iota(I32, (PARTS, wide), 0) == tensor, ids, 0), axis=0, keepdims=True)
    start = lax.broadcasted_iota(I32, (PARTS, wide), 0) * shard
    from_owner = (own >= start) & (own < start + shard)
    hits = jnp.concatenate([jnp.where(mine, 1.0, 0.0), jnp.where(from_owner, 1.0, 0.0)], axis=0)
    before = lax.broadcasted_iota(I32, (256, 256), 0)
    after = lax.broadcasted_iota(I32, (256, 256), 1)
    upper = jnp.where(before <= after, 1.0, 0.0).astype(BF16)
    seen = jnp.full((2 * PARTS, 1), -1.0, F32)
    rank_list = []
    for n in range(wide // 256):
        part = hits[:, n * 256 : (n + 1) * 256]
        rank_list.append(jnp.dot(part.astype(BF16), upper, preferred_element_type=F32) + seen)
        seen = seen + jnp.sum(part, axis=1, keepdims=True)
    ranks = jnp.concatenate(rank_list, axis=1)
    owner = lax.broadcasted_iota(I32, (PARTS, wide), 0).astype(F32) * float(slots)
    place = jnp.sum(jnp.where(from_owner, owner + ranks[PARTS:], 0.0), axis=0, keepdims=True)
    place_v[...] = jnp.broadcast_to(place, (8, wide)).astype(I32)
    rank_v[0] = jnp.where(mine, ranks[:PARTS], -1.0)
    rank_v[1] = jnp.where(mine, local - (local & 255), 0).astype(F32)
    rank_v[2] = jnp.where(mine, local & 255, 0).astype(F32)
    to_place = pltpu.make_async_copy(place_v, place_s, s_sem.at[0])
    to_place.start()

    p1_end = p1()
    q1_end = q1()

    slot = lax.broadcasted_iota(I32, (tab_v.shape[1], wide), 0).astype(F32)
    kind = lax.broadcasted_iota(I32, (8, wide), 0)

    def table_step(b, _):
        rank = rank_v[0, pl.ds(b, 1), :]
        info = jnp.where(kind == 0, rank_v[1, pl.ds(b, 1), :], jnp.where(kind == 1, rank_v[2, pl.ds(b, 1), :], 0.0))
        hot = jnp.where(slot == rank, 1.0, 0.0).astype(BF16)
        got = lax.dot_general(info.astype(BF16), hot, NT, preferred_element_type=F32)
        tab_v[pl.ds(b, 1), :] = (got[0:1, :] + got[1:2, :]).astype(I32)
        return 0

    lax.fori_loop(0, PARTS, table_step, 0)
    to_tab = pltpu.make_async_copy(tab_v, tab_s, s_sem.at[1])
    to_tab.start()

    p1_end()
    q1_end()
    p2 = gather_ring(lambda r, h: ht.at[0, r, pl.ds(h * two, two)], z, z_peer, 12)
    q2 = gather_ring(lambda r, h: ht.at[1, pl.ds(h * two, two), r], y, y_peer, 18)

    band = 32
    whole = shard // band

    def widen(at, size, best):
        part = logits_ref[pl.ds(at, size), :].astype(F32)
        for c in range(lane_parts):
            source[c, pl.ds(at, size), :] = part[:, c * 128 : (c + 1) * 128]
        return jnp.maximum(best, jnp.max(part.reshape(size // 8, 8, tokens), axis=0))

    best = lax.fori_loop(
        0, whole, lambda i, m: widen(pl.multiple_of(i * band, band), band, m), jnp.full((8, tokens), LOW, F32)
    )
    if shard > whole * band:
        best = widen(whole * band, shard - whole * band, best)
    peak_here = jnp.max(best, axis=0, keepdims=True)

    def sum_exp(at, size, acc):
        part = jnp.exp(logits_ref[pl.ds(at, size), :].astype(F32) - peak_here)
        return acc + jnp.sum(part.reshape(size // 8, 8, tokens), axis=0)

    acc = lax.fori_loop(
        0, whole, lambda i, a: sum_exp(pl.multiple_of(i * band, band), band, a), jnp.zeros((8, tokens), F32)
    )
    if shard > whole * band:
        acc = sum_exp(whole * band, shard - whole * band, acc)
    total_here = jnp.sum(acc, axis=0, keepdims=True)
    row8 = lax.broadcasted_iota(I32, (8, tokens), 0)
    ex1[tensor] = jnp.where(row8 == 0, peak_here, jnp.where(row8 == 1, total_here, 0.0))
    first = [
        remote(ex1.at[tensor], ex1.at[tensor], ex_send.at[0, i], ex_recv.at[0, i], group_peer(i))
        for i in range(1, PARTS)
    ]
    for copy in first:
        copy.start()

    to_tab.wait()
    to_place.wait()

    def pick(index_of, count):
        def go(i, _):
            for r in range(16):
                j = i * 16 + r
                at = jnp.clip(index_of(j), 0, source.shape[1] - 1)
                for c in range(lane_parts):
                    picked[c, pl.ds(j, 1), :] = source[c, pl.ds(at, 1), :]
            return 0

        lax.fori_loop(0, count // 16, go, 0)

    def joined(at, size):
        return jnp.concatenate([picked[c, pl.ds(at, size), :] for c in range(lane_parts)], axis=1)

    def sent(i):
        to = (tensor + i) % PARTS
        return remote(outgoing.at[to], incoming.at[tensor], a2a_send.at[i], a2a_recv.at[i], (dp, to))

    def send_step(i, _):
        to = (tensor + i) % PARTS
        pick(lambda j: tab_s[to, j], slots)
        outgoing[to] = joined(0, slots).astype(BF16)
        sent(i).start()
        return 0

    lax.fori_loop(1, two * RING, send_step, 0)
    p2_end = p2()
    q2_end = q2()
    lax.fori_loop(two * RING, PARTS, send_step, 0)
    pick(lambda j: tab_s[tensor, j], slots)
    incoming[tensor] = joined(0, slots).astype(BF16)

    p2_end()
    q2_end()
    swap_h = remote(
        ht.at[:, :, pl.ds((1 - core) * CORES, CORES)], h_peer, pair_send.at[0], pair_recv.at[0], partner
    )
    swap_h.start()

    pieces = PARTS * sub // chunk
    each = chunk // sub
    expo[...] = jnp.zeros((rows, both), F32)

    def score_step(i, _):
        w_copy(i).wait()
        for s in range(steps):
            at = i * each
            h = ht[s, at // RING, pl.ds(at % RING, each)].reshape(chunk, tokens)
            lanes = slice(s * tokens, (s + 1) * tokens)
            expo[0:block, lanes] += jnp.dot(w_buf[i % 2], h, preferred_element_type=F32)

        @pl.when(i + 2 < pieces)
        def _():
            w_copy(i + 2).start()

        return 0

    lax.fori_loop(0, pieces, score_step, 0)
    if rows > block:
        expo[block:rows, :] = jnp.full((rows - block, both), LOW, F32)

    def top_step(i, m):
        at = pl.multiple_of(i * band, band)
        return jnp.maximum(m, jnp.max(expo[pl.ds(at, band), :].reshape(band // 8, 8, both), axis=0))

    top = lax.fori_loop(0, rows // band, top_step, jnp.full((8, both), LOW, F32))
    top = jnp.max(top, axis=0, keepdims=True)

    def exp_step(i, a):
        at = pl.multiple_of(i * band, band)
        value = jnp.exp(expo[pl.ds(at, band), :] - top)
        expo[pl.ds(at, band), :] = value
        return a + jnp.sum(value.reshape(band // 8, 8, both), axis=0)

    weight = lax.fori_loop(0, rows // band, exp_step, jnp.zeros((8, both), F32))
    weight = jnp.sum(weight, axis=0, keepdims=True)

    own_rows = CORES * sub
    for i in range(RING):
        for s in range(steps):
            part = ht[s, i, pl.ds(core * CORES, CORES)].reshape(own_rows, tokens)
            hn_ref[i, s * tokens : (s + 1) * tokens, :] = part.T
    swap_h.wait()
    for i in range(RING):
        for s in range(steps):
            part = h_peer[s, i].reshape(own_rows, tokens)
            hn_ref[i, both + s * tokens : both + (s + 1) * tokens, :] = part.T

    for copy in first:
        copy.wait()
    peaks = [ex1[i, 0:1, :] for i in range(PARTS)]
    peak = functools.reduce(jnp.maximum, peaks)
    total = sum(ex1[i, 1:2, :] * jnp.exp(peaks[i] - peak) for i in range(PARTS))

    def arrived(i, _):
        sent(i).wait()
        return 0

    lax.fori_loop(1, PARTS, arrived, 0)

    def widen_in(i, _):
        part = incoming[i].astype(F32)
        for c in range(lane_parts):
            source[c, pl.ds(pl.multiple_of(i * slots, 16), slots), :] = part[:, c * 128 : (c + 1) * 128]
        return 0

    lax.fori_loop(0, PARTS, widen_in, 0)
    pick(lambda j: place_s[0, j], rows)

    def prob_step(i, a):
        at = pl.multiple_of(i * band, band)
        value = jnp.exp(joined(at, band) - peak) / total
        inside = lax.broadcasted_iota(I32, (band, tokens), 0) + at < block
        value = jnp.where(inside, value, 0.0).astype(BF16).astype(F32)
        probs[pl.ds(at, band), :] = value
        return a + jnp.sum(value.reshape(band // 8, 8, tokens), axis=0)

    mass_here = lax.fori_loop(0, rows // band, prob_step, jnp.zeros((8, tokens), F32))
    mass_here = jnp.sum(mass_here, axis=0, keepdims=True)

    row8 = lax.broadcasted_iota(I32, (8, both), 0)
    mass_wide = jnp.concatenate([mass_here] * steps, axis=1)
    ex2[tensor] = jnp.where(row8 == 0, top, jnp.where(row8 == 1, weight, jnp.where(row8 == 2, mass_wide, 0.0)))
    second = [
        remote(ex2.at[tensor], ex2.at[tensor], ex_send.at[1, i], ex_recv.at[1, i], group_peer(i))
        for i in range(1, PARTS)
    ]
    for copy in second:
        copy.start()
    for copy in second:
        copy.wait()
    tops = [ex2[i, 0:1, :] for i in range(PARTS)]
    top_all = functools.reduce(jnp.maximum, tops)
    weight_all = sum(ex2[i, 1:2, :] * jnp.exp(tops[i] - top_all) for i in range(PARTS))
    mass = sum(ex2[i, 2:3, 0:tokens] for i in range(PARTS))

    def shift(value, step):
        if step == 0:
            return value
        lane = lax.broadcasted_iota(I32, value.shape, 1)
        return jnp.where(lane < tokens - step, pltpu.roll(value, tokens - step, 1), 0.0)

    factor = jnp.exp(top - top_all) / weight_all
    scales = [LOSS_SCALE * STEP_DECAY**s for s in range(steps)]
    coefs = []
    for s in range(steps):
        moved = shift(jnp.broadcast_to(mass, (8, tokens)), s)[0:1, :]
        coefs.append(scales[s] * moved * factor[:, s * tokens : (s + 1) * tokens])

    def slope_step(i, _):
        at = pl.multiple_of(i * 16, 16)
        prob = probs[pl.ds(at, 16), :]
        for s in range(steps):
            value = expo[pl.ds(at, 16), s * tokens : (s + 1) * tokens] * coefs[s] - scales[s] * shift(prob, s)
            sl_ref[pl.ds(at, 16), s * tokens : (s + 1) * tokens] = value.astype(BF16)
        return 0

    swaps = []
    for n, (at, size) in enumerate(pieces_of(rows)):
        lax.fori_loop(at // 16, (at + size) // 16, slope_step, 0)
        swaps.append(
            remote(
                sl_ref.at[pl.ds(at, size), pl.ds(0, both)],
                sl_ref.at[pl.ds(at, size), pl.ds(both, both)],
                pair_send.at[1 + n],
                pair_recv.at[1 + n],
                partner,
            )
        )
        swaps[-1].start()
    for copy in swaps:
        copy.wait()


def front(hid, ids, logits, w, slots):
    steps, sub, tokens = hid.shape
    parts, block = ids.shape
    shard = logits.shape[0]
    both = steps * tokens
    rows = ceil_to(block, 32)
    wide = ceil_to(block, 256)
    depth = ceil_to(max(shard, parts * slots), 32)
    vmem = pl.BlockSpec(memory_space=pltpu.VMEM)
    return pl.pallas_call(
        functools.partial(front_kernel, (steps, tokens, block, rows, slots)),
        out_shape=(
            jax.ShapeDtypeStruct((rows, CORES * both), BF16),
            jax.ShapeDtypeStruct((RING, CORES * both, CORES * sub), BF16),
        ),
        in_specs=[vmem, vmem, vmem, pl.BlockSpec(memory_space=pl.ANY)],
        out_specs=(vmem, vmem),
        scratch_shapes=[
            pltpu.VMEM((steps, RING, RING, sub, tokens), BF16),
            pltpu.VMEM((steps, RING, CORES, sub, tokens), BF16),
            pltpu.VMEM((2, block, 2 * sub), BF16),
            pltpu.VMEM((tokens // 128, depth, 128), F32),
            pltpu.VMEM((tokens // 128, ceil_to(max(rows, slots), 16), 128), F32),
            pltpu.VMEM((parts, slots, tokens), BF16),
            pltpu.VMEM((parts, slots, tokens), BF16),
            pltpu.VMEM((rows, both), F32),
            pltpu.VMEM((rows, tokens), F32),
            pltpu.VMEM((3, parts, wide), F32),
            pltpu.VMEM((parts, ceil_to(slots, 128)), I32),
            pltpu.VMEM((8, wide), I32),
            pltpu.VMEM((parts, 8, tokens), F32),
            pltpu.VMEM((parts, 8, both), F32),
            pltpu.SMEM((parts, ceil_to(slots, 128)), I32),
            pltpu.SMEM((8, wide), I32),
            pltpu.SemaphoreType.DMA((24,)),
            pltpu.SemaphoreType.DMA((24,)),
            pltpu.SemaphoreType.DMA((parts,)),
            pltpu.SemaphoreType.DMA((parts,)),
            pltpu.SemaphoreType.DMA((2, parts)),
            pltpu.SemaphoreType.DMA((2, parts)),
            pltpu.SemaphoreType.DMA((5,)),
            pltpu.SemaphoreType.DMA((5,)),
            pltpu.SemaphoreType.DMA((2,)),
            pltpu.SemaphoreType.DMA((2,)),
        ],
        compiler_params=pltpu.CompilerParams(
            collective_id=2, has_side_effects=True, vmem_limit_bytes=62 * 2**20
        ),
        name="front",
    )(hid, ids, logits, w)


def sums_kernel(
    sizes,
    sl_ref,
    hn_ref,
    w_ref,
    gh_ref,
    gw_ref,
    flat,
    w_buf,
    terms,
    x_out,
    x_far,
    x_in,
    p_out,
    p_far,
    p_in,
    q_out,
    q_far,
    q_in,
    p2_out,
    p2_far,
    p2_in,
    q2_out,
    q2_far,
    q2_in,
    w_sem,
    ring_send,
    ring_recv,
):
    steps, tokens, block = sizes
    rows = sl_ref.shape[0]
    both = steps * tokens
    dp, tensor, x, core, z, y = places()
    sub = gh_ref.shape[1]
    chunk = w_buf.shape[2]

    def x_peer(by):
        return (((x + by) % RING) * CORES + core, tensor)

    def z_peer(by):
        return (dp, ((z + by) % RING) * RING + y)

    def y_peer(by):
        return (dp, z * RING + (y + by) % RING)

    per = RING * sub // chunk
    count = RING * per

    def w_row(i):
        order = (2, 1, RING - 1, 0)[i // per]
        return ((z + order) % RING) * per + i % per

    def w_copy(i):
        at = pl.multiple_of(w_row(i) * chunk, chunk)
        return pltpu.make_async_copy(w_ref.at[:, pl.ds(at, chunk)], w_buf.at[i % 2], w_sem.at[i % 2])

    w_copy(0).start()
    w_copy(1).start()

    barrier = pltpu.get_barrier_semaphore()
    for peer in (x_peer, y_peer, z_peer):
        for by in (1, RING - 1):
            pl.semaphore_signal(barrier, inc=1, device_id=peer(by), device_id_type=MESH)
    pl.semaphore_wait(barrier, 6)

    def link(n, src, dst, device):
        return remote(src, dst, ring_send.at[n], ring_recv.at[n], device)

    cuts = pieces_of(rows)
    half = rows // 2

    def head_part(by, at, size):
        return jnp.dot(sl_ref[at : at + size, :], hn_ref[(x + by) % RING], preferred_element_type=F32)

    def x_send(slot, by, h, into, to, base, far=None):
        copies = []
        for n in range(2):
            at, size = cuts[2 * h + n]
            value = head_part(by, at, size)
            spot = pl.ds(at - h * half, size)
            if far is not None:
                value = value + x_far[far, spot, :].astype(F32)
            x_out[slot, spot, :] = value.astype(BF16)
            copies.append(link(base + n, x_out.at[slot, spot], into.at[spot], x_peer(to)))
            copies[-1].start()
        return copies

    far_r = x_send(0, 2, 0, x_far.at[0], 1, 0)
    far_l = x_send(1, 2, 1, x_far.at[1], RING - 1, 2)
    free_r = x_send(3, 1, 1, x_in.at[1], 1, 4)
    free_l = x_send(4, RING - 1, 0, x_in.at[2], RING - 1, 6)

    for at in range(0, rows, 128):
        size = min(128, rows - at)
        flat[:, at : at + size] = sl_ref[at : at + size, 0:both].T

    def term_step(i):
        w_copy(i).wait()
        value = jnp.dot(flat[:, 0:block], w_buf[i % 2], preferred_element_type=F32)
        first = w_row(i) * (chunk // sub)
        flipped = value.T
        for n in range(chunk // sub):
            terms[first + n] = flipped[n * sub : (n + 1) * sub, :]
        if i + 2 < count:
            w_copy(i + 2).start()

    pair_of = RING // 2
    p_at, q_at = pl.ds(0, tokens), pl.ds(tokens, tokens)

    def p_term(by, n):
        return terms[((z + by) % RING) * RING + n, :, p_at]

    def q_term(by, n):
        return terms[n * RING + (y + by) % RING, :, q_at]

    def ring_sum(part, out, far, into, peer, base):
        def put(slot, by, h, extra=None):
            for n, value in enumerate(part(by, h)):
                if extra is not None:
                    value = value + extra[n].astype(F32)
                out[slot, n] = value.astype(BF16)

        def start(n, slot, dst, by):
            copy = link(base + n, out.at[slot], dst, peer(by))
            copy.start()
            return copy

        held = {}

        def begin():
            put(0, 2, 0)
            held["a"] = start(0, 0, far.at[0], 1)
            put(1, 2, 1)
            held["b"] = start(1, 1, far.at[1], RING - 1)

        def free():
            put(3, 1, 1)
            held["c"] = start(2, 3, into.at[1], 1)
            put(4, RING - 1, 0)
            held["d"] = start(3, 4, into.at[2], RING - 1)

        def late():
            held["a"].wait()
            put(2, 1, 0, far.at[0])
            held["e"] = start(4, 2, into.at[0], 1)
            held["b"].wait()
            put(5, RING - 1, 1, far.at[1])
            held["f"] = start(5, 5, into.at[3], RING - 1)

        def end():
            for name in "cdef":
                held[name].wait()

        return begin, free, late, end

    def p_part(by, h):
        return [p_term(by, h * pair_of + n) for n in range(pair_of)]

    def q_part(by, h):
        return [q_term(by, h * pair_of + n) for n in range(pair_of)]

    p_begin, p_free, p_late, p_end = ring_sum(p_part, p_out, p_far, p_in, z_peer, 12)
    q_begin, q_free, q_late, q_end = ring_sum(q_part, q_out, q_far, q_in, y_peer, 18)
    for i in range(count):
        term_step(i)
        if i + 1 == per:
            p_begin()
        if i + 1 == 3 * per:
            p_free()
    q_begin()
    q_free()
    p_late()
    q_late()

    for copy in far_r:
        copy.wait()
    dep_r = x_send(2, 1, 0, x_in.at[0], 1, 8, far=0)
    for copy in far_l:
        copy.wait()
    dep_l = x_send(5, RING - 1, 1, x_in.at[3], RING - 1, 10, far=1)

    for at, size in cuts:
        keep = min(size, block - at)
        gw_ref[at : at + keep, :] = head_part(0, at, size)[0:keep]

    p_end()
    for n in range(RING):
        got = p_in[n // pair_of, n % pair_of].astype(F32) + p_in[2 + n // pair_of, n % pair_of].astype(F32)
        mine = z * RING + n
        terms[mine, :, p_at] = terms[mine, :, p_at] + got
    q_end()
    for n in range(RING):
        got = q_in[n // pair_of, n % pair_of].astype(F32) + q_in[2 + n // pair_of, n % pair_of].astype(F32)
        mine = n * RING + y
        terms[mine, :, q_at] = terms[mine, :, q_at] + got

    cut = sub // 2

    def p2_part(by, h):
        return [terms[z * RING + (y + by) % RING, h * cut : (h + 1) * cut, p_at]]

    def q2_part(by, h):
        return [terms[((z + by) % RING) * RING + y, h * cut : (h + 1) * cut, q_at]]

    p2 = ring_sum(p2_part, p2_out, p2_far, p2_in, y_peer, 24)
    q2 = ring_sum(q2_part, q2_out, q2_far, q2_in, z_peer, 30)
    for stage in range(4):
        p2[stage]()
        q2[stage]()
    for s, (lane, into) in enumerate(((p_at, p2_in), (q_at, q2_in))):
        for h in range(2):
            value = terms[tensor, h * cut : (h + 1) * cut, lane]
            value = value + into[h, 0].astype(F32) + into[2 + h, 0].astype(F32)
            gh_ref[s, h * cut : (h + 1) * cut, :] = value.astype(BF16)

    def add_in(at, size, h):
        to = at + h * half
        got = x_in[h, pl.ds(at, size), :].astype(F32) + x_in[2 + h, pl.ds(at, size), :].astype(F32)
        keep = min(size, block - to)
        gw_ref[to : to + keep, :] = gw_ref[to : to + keep, :] + got[0:keep]

    for h, from_left, from_right in ((0, dep_r, free_l), (1, free_r, dep_l)):
        for n in range(2):
            from_left[n].wait()
            from_right[n].wait()
            at, size = cuts[2 * h + n]
            for i in range(0, size, 16):
                add_in(at - h * half + i, 16, h)


def sums(sl, hn, w, steps, tokens, block):
    rows = sl.shape[0]
    d = w.shape[1]
    sub = d // PARTS
    both = steps * tokens
    width = CORES * sub
    half = rows // 2
    vmem = pl.BlockSpec(memory_space=pltpu.VMEM)
    ring_x = [(6, half, width), (2, half, width), (4, half, width)]
    ring_1 = [(6, 2, sub, tokens), (2, 2, sub, tokens), (4, 2, sub, tokens)]
    ring_2 = [(6, 1, sub // 2, tokens), (2, 1, sub // 2, tokens), (4, 1, sub // 2, tokens)]
    return pl.pallas_call(
        functools.partial(sums_kernel, (steps, tokens, block)),
        out_shape=(
            jax.ShapeDtypeStruct((steps, sub, tokens), BF16),
            jax.ShapeDtypeStruct((block, width), F32),
        ),
        in_specs=[vmem, vmem, pl.BlockSpec(memory_space=pl.ANY)],
        out_specs=(vmem, vmem),
        scratch_shapes=[
            pltpu.VMEM((both, ceil_to(rows, 128)), BF16),
            pltpu.VMEM((2, block, 2 * sub), BF16),
            pltpu.VMEM((PARTS, sub, both), F32),
        ]
        + [pltpu.VMEM(shape, BF16) for shape in ring_x + ring_1 + ring_1 + ring_2 + ring_2]
        + [
            pltpu.SemaphoreType.DMA((2,)),
            pltpu.SemaphoreType.DMA((36,)),
            pltpu.SemaphoreType.DMA((36,)),
        ],
        compiler_params=pltpu.CompilerParams(
            collective_id=3, has_side_effects=True, vmem_limit_bytes=62 * 2**20
        ),
        name="sums",
    )(sl, hn, w)


def per_device(hidden, draft_head, target_logits, draft_to_target):
    steps, tokens, _ = hidden.shape
    block = draft_to_target.shape[0] // PARTS
    heavy = block // 8
    bound = heavy + (block - heavy + PARTS - 1) // PARTS
    slots = ceil_to(bound, 16)
    w = draft_head.T
    sl, hn = front(hidden.transpose(0, 2, 1), draft_to_target.reshape(PARTS, block), target_logits.T, w, slots)
    gh, gw = sums(sl, hn, w, steps, tokens, block)
    return gh.transpose(0, 2, 1), gw.T


def solution(mesh):
    in_specs = (P(None, "dp", "tensor"), P(None, "tensor"), P("dp", "tensor"), P())
    out_specs = (P(None, "dp", "tensor"), P("dp", "tensor"))
    return jax.shard_map(
        per_device, mesh=mesh, in_specs=in_specs, out_specs=out_specs, check_vma=False
    )
```

time: 730 us -> 191 us (0.26); the launches traced: 721 us -> 190 us
  waiting for transfers between devices: 273 us -> 0 us
  Pallas kernels: 0 us -> 182 us
  other arithmetic: 149 us -> 0 us
  local copies, waits for them, and re-layouts: 145 us -> 7.6 us
  blocking collectives: 93.1 us -> 0 us
  matrix products: 42.8 us -> 0 us
  between operations: 14 us -> 0.65 us
    reduce_scatter x2 -> x0, waiting for transfers between devices: 252 us -> none  [the longest x1 159 us: per_device(): lax.psum_scatter(jnp.einsum('stc,stv->cv', h_full, slopes, preferred_elem...]
    pallas_call x0 -> x2, Pallas kernels: none -> 182 us  [the longest x1 107 us: front(): pl.pallas_call(functools.partial(front_kernel, (steps, tokens, block, row...]
    another operation x5 -> x0, other arithmetic: 128 us -> none
    scatter x1 -> x0, local copies, waits for them, and re-layouts: 111 us -> none  [per_device(): table = jnp.zeros((parts * bound,), jnp.int32).at[placing.reshape(-1)].se...]
    psum x2 -> x0, blocking collectives: 57.5 us -> none  [per_device(): lax.psum((jnp.sum(jnp.exp(logits - tpeak[:, None]), axis=1), jnp.sum(jnp....]
    dot_general x3 -> x0, matrix products: 42.8 us -> none  [the longest x1 16.1 us: per_device(): jnp.einsum('stc,stv->cv', h_full, slopes, preferred_element_type=jnp.floa...]
    pmax x1 -> x0, blocking collectives: 35.5 us -> none  [per_device(): tpeak, dpeak = lax.pmax((tpeak_local, dpeak_local), 'tensor')]
    gather x3 -> x0, local copies, waits for them, and re-layouts: 22.9 us -> none  [the longest x2 17.9 us: per_device(): outgoing = jnp.take(owned_probs, table, axis=1)]
  transfers between devices with their start and end apart: 4 -> 0, of which waited for: 3 -> 0; matrix products, arithmetic and copies ran while one was open for 37% -> 0% of each run, Pallas kernels for 0% -> 0%
where the time goes in v2:
time: 191 us; the launch traced here: 190 us
  Pallas kernels  182 us (95%)
  local copies, waits for them, and re-layouts  7.6 us (4%)
    pallas_call x1, Pallas kernels, front(): pl.pallas_call(functools.partial(front_kernel, (steps, tokens, block, row...  107 us
    pallas_call x1, Pallas kernels, sums(): pl.pallas_call(functools.partial(sums_kernel, (steps, tokens, block)), ou...  74.9 us
    unnamed x2, local copies, waits for them, and re-layouts  5.95 us

profile of v2, /device:TPU:1, one launch (start us, length us, event | category | flops | bytes accessed | tf_op | source)
XLA Modules:
  0.0 190.1 jit_solution(1869636165273520820)
XLA Ops:
  0.6 1.6 reshape.7.ids_ref
  2.3 106.9 %front.1 = (bf16[1504,1024]{1,0:T(8,128)(2,1)}, bf16[4,1024,640]{2,1,0:T(8,128)(2,1)}) custom-call(bf16[2,320,256]{2,1,0:T(8,128)(2,1)} %bitcast.10, s32[16,1500]{1,0:T(8,128)} %reshape.7.ids_ref, bf16[9496,256]{1,0:T(8,128)(2,1)} %bitcast.7, bf16[1500,5120]{1,0:T(8,128)(2,1)} %bitcast.5), custom_call_target="tpu_custom_call" | custom-call | tf_op jit(solution)/shard_map/front/pallas_call | solution.py:423
  109.2 74.9 %sums.1 = (bf16[2,320,256]{2,1,0:T(8,128)(2,1)}, f32[1500,640]{1,0:T(8,128)}) custom-call(bf16[1504,1024]{1,0:T(8,128)(2,1)} %get-tuple-element.6.sl_ref, bf16[4,1024,640]{2,1,0:T(8,128)(2,1)} %get-tuple-element.7.hn_ref, bf16[1500,5120]{1,0:T(8,128)(2,1)} %bitcast.6), custom_call_target="tpu_custom_call" | custom-call | tf_op jit(solution)/shard_map/sums/pallas_call | solution.py:707
  184.1 1.7 copy.8
  185.8 4.2 %copy.9 = f32[640,1500]{0,1:T(8,128)} copy(f32[640,1500]{0,1:T(8,128)} %bitcast.8) | data formatting | bytes 7680000

commit v3 on v2

--- a/solution.py
+++ b/solution.py
@@ -30,6 +30,18 @@
     x, core = dp // CORES, dp % CORES
     z, y = tensor // RING, tensor % RING
     return dp, tensor, x, core, z, y
+
+
+def sweep(first, last, size, step, carry):
+    full = (last - first) // size
+
+    def go(i, value):
+        return step(pl.multiple_of(first + i * size, 16), size, value)
+
+    carry = lax.fori_loop(0, full, go, carry)
+    if first + full * size < last:
+        carry = step(first + full * size, last - first - full * size, carry)
+    return carry
 
 
 def remote(src, dst, send, recv, device):
@@ -150,6 +162,30 @@
     p1 = gather_ring(lambda r, h: half_rows(0, z, r, h), y, y_peer, 0)
     q1 = gather_ring(lambda r, h: half_rows(1, r, y, h), z, z_peer, 6)
 
+    def top_rows(at, size, best):
+        part = logits_ref[pl.ds(at, size), :].astype(F32)
+        return jnp.maximum(best, jnp.max(part.reshape(size // 8, 8, tokens), axis=0))
+
+    best = sweep(0, shard, 64, top_rows, jnp.full((8, tokens), LOW, F32))
+    peak_here = jnp.max(best, axis=0, keepdims=True)
+
+    def exp_rows(at, size, acc):
+        part = jnp.exp(logits_ref[pl.ds(at, size), :].astype(F32) - peak_here)
+        for c in range(lane_parts):
+            source[c, pl.ds(at, size), :] = part[:, c * 128 : (c + 1) * 128]
+        return acc + jnp.sum(part.reshape(size // 8, 8, tokens), axis=0)
+
+    acc = sweep(0, shard, 64, exp_rows, jnp.zeros((8, tokens), F32))
+    total_here = jnp.sum(acc, axis=0, keepdims=True)
+    row8 = lax.broadcasted_iota(I32, (8, tokens), 0)
+    ex1[tensor] = jnp.where(row8 == 0, peak_here, jnp.where(row8 == 1, total_here, 0.0))
+    first = [
+        remote(ex1.at[tensor], ex1.at[tensor], ex_send.at[0, i], ex_recv.at[0, i], group_peer(i))
+        for i in range(1, PARTS)
+    ]
+    for copy in first:
+        copy.start()
+
     ids = jnp.concatenate([ids_ref[...], jnp.full((PARTS, wide - block), -1, I32)], axis=1)
     local = ids - tensor * shard
     mine = (local >= 0) & (local < shard)
@@ -169,7 +205,7 @@
     ranks = jnp.concatenate(rank_list, axis=1)
     owner = lax.broadcasted_iota(I32, (PARTS, wide), 0).astype(F32) * float(slots)
     place = jnp.sum(jnp.where(from_owner, owner + ranks[PARTS:], 0.0), axis=0, keepdims=True)
-    place_v[...] = jnp.broadcast_to(place, (8, wide)).astype(I32)
+    place_v[...] = jnp.clip(jnp.broadcast_to(place, (8, wide)).astype(I32), 0, PARTS * slots - 1)
     rank_v[0] = jnp.where(mine, ranks[:PARTS], -1.0)
     rank_v[1] = jnp.where(mine, local - (local & 255), 0).astype(F32)
     rank_v[2] = jnp.where(mine, local & 255, 0).astype(F32)
@@ -187,63 +223,37 @@
         info = jnp.where(kind == 0, rank_v[1, pl.ds(b, 1), :], jnp.where(kind == 1, rank_v[2, pl.ds(b, 1), :], 0.0))
         hot = jnp.where(slot == rank, 1.0, 0.0).astype(BF16)
         got = lax.dot_general(info.astype(BF16), hot, NT, preferred_element_type=F32)
-        tab_v[pl.ds(b, 1), :] = (got[0:1, :] + got[1:2, :]).astype(I32)
+        found = (got[0:1, :] + got[1:2, :]).astype(I32)
+        tab_v[pl.ds(b, 1), :] = jnp.clip(found, 0, shard - 1)
         return 0
 
-    lax.fori_loop(0, PARTS, table_step, 0)
-    to_tab = pltpu.make_async_copy(tab_v, tab_s, s_sem.at[1])
-    to_tab.start()
-
+    lax.fori_loop(0, two, table_step, 0)
     p1_end()
     q1_end()
     p2 = gather_ring(lambda r, h: ht.at[0, r, pl.ds(h * two, two)], z, z_peer, 12)
     q2 = gather_ring(lambda r, h: ht.at[1, pl.ds(h * two, two), r], y, y_peer, 18)
-
-    band = 32
-    whole = shard // band
-
-    def widen(at, size, best):
-        part = logits_ref[pl.ds(at, size), :].astype(F32)
-        for c in range(lane_parts):
-            source[c, pl.ds(at, size), :] = part[:, c * 128 : (c + 1) * 128]
-        return jnp.maximum(best, jnp.max(part.reshape(size // 8, 8, tokens), axis=0))
-
-    best = lax.fori_loop(
-        0, whole, lambda i, m: widen(pl.multiple_of(i * band, band), band, m), jnp.full((8, tokens), LOW, F32)
-    )
-    if shard > whole * band:
-        best = widen(whole * band, shard - whole * band, best)
-    peak_here = jnp.max(best, axis=0, keepdims=True)
-
-    def sum_exp(at, size, acc):
-        part = jnp.exp(logits_ref[pl.ds(at, size), :].astype(F32) - peak_here)
-        return acc + jnp.sum(part.reshape(size // 8, 8, tokens), axis=0)
-
-    acc = lax.fori_loop(
-        0, whole, lambda i, a: sum_exp(pl.multiple_of(i * band, band), band, a), jnp.zeros((8, tokens), F32)
-    )
-    if shard > whole * band:
-        acc = sum_exp(whole * band, shard - whole * band, acc)
-    total_here = jnp.sum(acc, axis=0, keepdims=True)
-    row8 = lax.broadcasted_iota(I32, (8, tokens), 0)
-    ex1[tensor] = jnp.where(row8 == 0, peak_here, jnp.where(row8 == 1, total_here, 0.0))
-    first = [
-        remote(ex1.at[tensor], ex1.at[tensor], ex_send.at[0, i], ex_recv.at[0, i], group_peer(i))
-        for i in range(1, PARTS)
-    ]
+    lax.fori_loop(two, PARTS, table_step, 0)
+    to_tab = pltpu.make_async_copy(tab_v, tab_s, s_sem.at[1])
+    to_tab.start()
+
     for copy in first:
-        copy.start()
-
+        copy.wait()
+    peaks = [ex1[i, 0:1, :] for i in range(PARTS)]
+    peak = functools.reduce(jnp.maximum, peaks)
+    total = sum(ex1[i, 1:2, :] * jnp.exp(peaks[i] - peak) for i in range(PARTS))
+    share = jnp.exp(peak_here - peak) / total
     to_tab.wait()
     to_place.wait()
 
     def pick(index_of, count):
         def go(i, _):
+            got = []
             for r in range(16):
-                j = i * 16 + r
-                at = jnp.clip(index_of(j), 0, source.shape[1] - 1)
+                at = index_of(i * 16 + r)
+                got.append([source[c, pl.ds(at, 1), :] for c in range(lane_parts)])
+            for r in range(16):
                 for c in range(lane_parts):
-                    picked[c, pl.ds(j, 1), :] = source[c, pl.ds(at, 1), :]
+                    picked[c, pl.ds(i * 16 + r, 1), :] = got[r][c]
             return 0
 
         lax.fori_loop(0, count // 16, go, 0)
@@ -258,7 +268,7 @@
     def send_step(i, _):
         to = (tensor + i) % PARTS
         pick(lambda j: tab_s[to, j], slots)
-        outgoing[to] = joined(0, slots).astype(BF16)
+        outgoing[to] = (joined(0, slots) * share).astype(BF16)
         sent(i).start()
         return 0
 
@@ -267,7 +277,7 @@
     q2_end = q2()
     lax.fori_loop(two * RING, PARTS, send_step, 0)
     pick(lambda j: tab_s[tensor, j], slots)
-    incoming[tensor] = joined(0, slots).astype(BF16)
+    incoming[tensor] = (joined(0, slots) * share).astype(BF16)
 
     p2_end()
     q2_end()
@@ -298,20 +308,18 @@
     if rows > block:
         expo[block:rows, :] = jnp.full((rows - block, both), LOW, F32)
 
-    def top_step(i, m):
-        at = pl.multiple_of(i * band, band)
-        return jnp.maximum(m, jnp.max(expo[pl.ds(at, band), :].reshape(band // 8, 8, both), axis=0))
-
-    top = lax.fori_loop(0, rows // band, top_step, jnp.full((8, both), LOW, F32))
+    def top_step(at, size, m):
+        return jnp.maximum(m, jnp.max(expo[pl.ds(at, size), :].reshape(size // 8, 8, both), axis=0))
+
+    top = sweep(0, rows, 32, top_step, jnp.full((8, both), LOW, F32))
     top = jnp.max(top, axis=0, keepdims=True)
 
-    def exp_step(i, a):
-        at = pl.multiple_of(i * band, band)
-        value = jnp.exp(expo[pl.ds(at, band), :] - top)
-        expo[pl.ds(at, band), :] = value
-        return a + jnp.sum(value.reshape(band // 8, 8, both), axis=0)
-
-    weight = lax.fori_loop(0, rows // band, exp_step, jnp.zeros((8, both), F32))
+    def exp_step(at, size, a):
+        value = jnp.exp(expo[pl.ds(at, size), :] - top)
+        expo[pl.ds(at, size), :] = value
+        return a + jnp.sum(value.reshape(size // 8, 8, both), axis=0)
+
+    weight = sweep(0, rows, 32, exp_step, jnp.zeros((8, both), F32))
     weight = jnp.sum(weight, axis=0, keepdims=True)
 
     own_rows = CORES * sub
@@ -325,36 +333,28 @@
             part = h_peer[s, i].reshape(own_rows, tokens)
             hn_ref[i, both + s * tokens : both + (s + 1) * tokens, :] = part.T
 
-    for copy in first:
-        copy.wait()
-    peaks = [ex1[i, 0:1, :] for i in range(PARTS)]
-    peak = functools.reduce(jnp.maximum, peaks)
-    total = sum(ex1[i, 1:2, :] * jnp.exp(peaks[i] - peak) for i in range(PARTS))
-
-    def arrived(i, _):
-        sent(i).wait()
-        return 0
-
-    lax.fori_loop(1, PARTS, arrived, 0)
-
-    def widen_in(i, _):
+    def widen_in(i):
         part = incoming[i].astype(F32)
         for c in range(lane_parts):
             source[c, pl.ds(pl.multiple_of(i * slots, 16), slots), :] = part[:, c * 128 : (c + 1) * 128]
+
+    widen_in(tensor)
+
+    def arrived(i, _):
+        sent(i).wait()
+        widen_in((tensor + PARTS - i) % PARTS)
         return 0
 
-    lax.fori_loop(0, PARTS, widen_in, 0)
+    lax.fori_loop(1, PARTS, arrived, 0)
     pick(lambda j: place_s[0, j], rows)
-
-    def prob_step(i, a):
-        at = pl.multiple_of(i * band, band)
-        value = jnp.exp(joined(at, band) - peak) / total
-        inside = lax.broadcasted_iota(I32, (band, tokens), 0) + at < block
-        value = jnp.where(inside, value, 0.0).astype(BF16).astype(F32)
-        probs[pl.ds(at, band), :] = value
-        return a + jnp.sum(value.reshape(band // 8, 8, tokens), axis=0)
-
-    mass_here = lax.fori_loop(0, rows // band, prob_step, jnp.zeros((8, tokens), F32))
+    if rows > block:
+        for c in range(lane_parts):
+            picked[c, block:rows, :] = jnp.zeros((rows - block, 128), F32)
+
+    def mass_step(at, size, a):
+        return a + jnp.sum(joined(at, size).reshape(size // 8, 8, tokens), axis=0)
+
+    mass_here = sweep(0, rows, 96, mass_step, jnp.zeros((8, tokens), F32))
     mass_here = jnp.sum(mass_here, axis=0, keepdims=True)
 
     row8 = lax.broadcasted_iota(I32, (8, both), 0)
@@ -366,6 +366,22 @@
     ]
     for copy in second:
         copy.start()
+
+    scales = [LOSS_SCALE * STEP_DECAY**s for s in range(steps)]
+
+    def shift(value, step):
+        if step == 0:
+            return value
+        lane = lax.broadcasted_iota(I32, value.shape, 1)
+        return jnp.where(lane < tokens - step, pltpu.roll(value, tokens - step, 1), 0.0)
+
+    def shift_step(at, size, _):
+        value = joined(at, size)
+        for s in range(steps):
+            probs[s, pl.ds(at, size), :] = scales[s] * shift(value, s)
+        return 0
+
+    sweep(0, rows, 96, shift_step, 0)
     for copy in second:
         copy.wait()
     tops = [ex2[i, 0:1, :] for i in range(PARTS)]
@@ -373,30 +389,22 @@
     weight_all = sum(ex2[i, 1:2, :] * jnp.exp(tops[i] - top_all) for i in range(PARTS))
     mass = sum(ex2[i, 2:3, 0:tokens] for i in range(PARTS))
 
-    def shift(value, step):
-        if step == 0:
-            return value
-        lane = lax.broadcasted_iota(I32, value.shape, 1)
-        return jnp.where(lane < tokens - step, pltpu.roll(value, tokens - step, 1), 0.0)
-
     factor = jnp.exp(top - top_all) / weight_all
-    scales = [LOSS_SCALE * STEP_DECAY**s for s in range(steps)]
     coefs = []
     for s in range(steps):
         moved = shift(jnp.broadcast_to(mass, (8, tokens)), s)[0:1, :]
         coefs.append(scales[s] * moved * factor[:, s * tokens : (s + 1) * tokens])
 
-    def slope_step(i, _):
-        at = pl.multiple_of(i * 16, 16)
-        prob = probs[pl.ds(at, 16), :]
+    def slope_step(at, size, _):
         for s in range(steps):
-            value = expo[pl.ds(at, 16), s * tokens : (s + 1) * tokens] * coefs[s] - scales[s] * shift(prob, s)
-            sl_ref[pl.ds(at, 16), s * tokens : (s + 1) * tokens] = value.astype(BF16)
+            lanes = slice(s * tokens, (s + 1) * tokens)
+            value = expo[pl.ds(at, size), lanes] * coefs[s] - probs[s, pl.ds(at, size), :]
+            sl_ref[pl.ds(at, size), lanes] = value.astype(BF16)
         return 0
 
     swaps = []
     for n, (at, size) in enumerate(pieces_of(rows)):
-        lax.fori_loop(at // 16, (at + size) // 16, slope_step, 0)
+        sweep(at, at + size, 96, slope_step, 0)
         swaps.append(
             remote(
                 sl_ref.at[pl.ds(at, size), pl.ds(0, both)],
@@ -437,7 +445,7 @@
             pltpu.VMEM((parts, slots, tokens), BF16),
             pltpu.VMEM((parts, slots, tokens), BF16),
             pltpu.VMEM((rows, both), F32),
-            pltpu.VMEM((rows, tokens), F32),
+            pltpu.VMEM((steps, rows, tokens), F32),
             pltpu.VMEM((3, parts, wide), F32),
             pltpu.VMEM((parts, ceil_to(slots, 128)), I32),
             pltpu.VMEM((8, wide), I32),

time: 191 us -> 181 us (0.948)
  Pallas kernels: 182 us -> 173 us
    pallas_call x1, Pallas kernels: 107 us -> 97.6 us  [front(): pl.pallas_call(functools.partial(front_kernel, (steps, tokens, block, row...]
where the time goes in v3:
time: 181 us
  Pallas kernels  173 us (96%)
  local copies, waits for them, and re-layouts  7.6 us (4%)
    pallas_call x1, Pallas kernels, front(): pl.pallas_call(functools.partial(front_kernel, (steps, tokens, block, row...  97.6 us
    pallas_call x1, Pallas kernels, sums(): pl.pallas_call(functools.partial(sums_kernel, (steps, tokens, block)), ou...  74.9 us
    unnamed x2, local copies, waits for them, and re-layouts  5.95 us

profile of v3, /device:TPU:1, one launch (start us, length us, event | category | flops | bytes accessed | tf_op | source)
XLA Modules:
  0.0 180.8 jit_solution(3934329131221272685)
XLA Ops:
  0.6 1.6 reshape.7.ids_ref
  2.3 97.6 %front.1 = (bf16[1504,1024]{1,0:T(8,128)(2,1)}, bf16[4,1024,640]{2,1,0:T(8,128)(2,1)}) custom-call(bf16[2,320,256]{2,1,0:T(8,128)(2,1)} %bitcast.10, s32[16,1500]{1,0:T(8,128)} %reshape.7.ids_ref, bf16[9496,256]{1,0:T(8,128)(2,1)} %bitcast.7, bf16[1500,5120]{1,0:T(8,128)(2,1)} %bitcast.5), custom_call_target="tpu_custom_call" | custom-call | tf_op jit(solution)/shard_map/front/pallas_call | solution.py:431
  99.9 74.9 %sums.1 = (bf16[2,320,256]{2,1,0:T(8,128)(2,1)}, f32[1500,640]{1,0:T(8,128)}) custom-call(bf16[1504,1024]{1,0:T(8,128)(2,1)} %get-tuple-element.6.sl_ref, bf16[4,1024,640]{2,1,0:T(8,128)(2,1)} %get-tuple-element.7.hn_ref, bf16[1500,5120]{1,0:T(8,128)(2,1)} %bitcast.6), custom_call_target="tpu_custom_call" | custom-call | tf_op jit(solution)/shard_map/sums/pallas_call | solution.py:715
  174.8 1.7 copy.8
  176.5 4.2 %copy.9 = f32[640,1500]{0,1:T(8,128)} copy(f32[640,1500]{0,1:T(8,128)} %bitcast.8) | data formatting | bytes 7680000

commit v4 on v3

v4 whole, which is shorter than its diff:
```python
import functools

import jax
import jax.numpy as jnp
from jax import lax
from jax.experimental import pallas as pl
from jax.experimental.pallas import tpu as pltpu
from jax.sharding import PartitionSpec as P

LOSS_SCALE = 256.0
STEP_DECAY = 0.8
MESH = pl.DeviceIdType.MESH
F32 = jnp.float32
BF16 = jnp.bfloat16
I32 = jnp.int32
RING = 4
CORES = 2
PARTS = RING * RING
LOW = -3.0e38
HELD = 4
NT = (((1,), (1,)), ((), ()))


def ceil_to(value, unit):
    return (value + unit - 1) // unit * unit


def places():
    dp = lax.axis_index("dp")
    tensor = lax.axis_index("tensor")
    x, core = dp // CORES, dp % CORES
    z, y = tensor // RING, tensor % RING
    return dp, tensor, x, core, z, y


def sweep(first, last, size, step, carry):
    full = (last - first) // size

    def go(i, value):
        return step(pl.multiple_of(first + i * size, 16), size, value)

    carry = lax.fori_loop(0, full, go, carry)
    if first + full * size < last:
        carry = step(first + full * size, last - first - full * size, carry)
    return carry


def remote(src, dst, send, recv, device):
    return pltpu.make_async_remote_copy(
        src_ref=src, dst_ref=dst, send_sem=send, recv_sem=recv, device_id=device, device_id_type=MESH
    )


def pieces_of(rows):
    half = rows // 2
    first = ceil_to(half // 2, 16)
    return [(0, first), (first, half - first), (half, first), (half + first, half - first)]


def kernel(
    sizes,
    hid_ref,
    ids_ref,
    logits_hbm,
    w_ref,
    gh_ref,
    gw_ref,
    tiles,
    arena,
    floats,
    hn,
    sl,
    w_buf,
    picked,
    expo,
    moved,
    flat,
    rank_v,
    tab_v,
    place_v,
    ex1,
    ex2,
    x_out,
    x_far,
    x_in,
    tab_s,
    place_s,
    ag_send,
    ag_recv,
    a2a_send,
    a2a_recv,
    ex_send,
    ex_recv,
    pair_send,
    pair_recv,
    w_sem,
    s_sem,
    ring_send,
    ring_recv,
):
    logits_in = pltpu.make_async_copy(logits_hbm, arena, s_sem.at[2])
    logits_in.start()
    steps, tokens, block, rows, slots = sizes
    shard = arena.shape[0]
    sub = hid_ref.shape[1]
    both = steps * tokens
    wide = ceil_to(block, 256)
    lane_parts = tokens // 128
    dp, tensor, x, core, z, y = places()
    partner = (x * CORES + 1 - core, tensor)

    def x_peer(by):
        return (((x + by) % RING) * CORES + core, tensor)

    def z_peer(by):
        return (dp, ((z + by) % RING) * RING + y)

    def y_peer(by):
        return (dp, z * RING + (y + by) % RING)

    def group_peer(i):
        return (dp, (tensor + i) % PARTS)

    chunk = w_buf.shape[2]

    def w_copy(i):
        return pltpu.make_async_copy(w_ref.at[:, pl.ds(i * chunk, chunk)], w_buf.at[i % 2], w_sem.at[i % 2])

    w_copy(0).start()
    w_copy(1).start()
    for s in range(steps):
        tiles[s, z, y] = hid_ref[s]

    barrier = pltpu.get_barrier_semaphore()
    for i in range(1, PARTS):
        pl.semaphore_signal(barrier, inc=1, device_id=group_peer(i), device_id_type=MESH)
    pl.semaphore_signal(barrier, inc=1, device_id=partner, device_id_type=MESH)
    for by in (1, RING - 1):
        pl.semaphore_signal(barrier, inc=1, device_id=x_peer(by), device_id_type=MESH)
    pl.semaphore_wait(barrier, PARTS + 2)

    def gather_ring(half, at, peer, base):
        right, left = (at + 1) % RING, (at + RING - 1) % RING

        def copy(n, r, h, by):
            ref = half(r, h)
            return remote(ref, ref, ag_send.at[base + n], ag_recv.at[base + n], peer(by))

        r1 = copy(0, at, 0, 1)
        l1 = copy(1, at, 1, RING - 1)
        r2 = copy(2, at, 1, 1)
        l2 = copy(3, at, 0, RING - 1)
        for c in (r1, l1, r2, l2):
            c.start()

        def pass_on():
            r1.wait()
            r3 = copy(4, left, 0, 1)
            r3.start()
            l1.wait()
            l3 = copy(5, right, 1, RING - 1)
            l3.start()

            def finish():
                for c in (r2, l2, r3, l3):
                    c.wait()

            return finish

        return pass_on

    def half_rows(s, at_z, at_y, h):
        return tiles.at[s, at_z, at_y, pl.ds(h * (sub // 2), sub // 2)]

    two = RING // 2
    p1 = gather_ring(lambda r, h: half_rows(0, z, r, h), y, y_peer, 0)
    q1 = gather_ring(lambda r, h: half_rows(1, r, y, h), z, z_peer, 6)

    def top_rows(at, size, best):
        part = arena[pl.ds(at, size), :].astype(F32)
        return jnp.maximum(best, jnp.max(part.reshape(size // 8, 8, tokens), axis=0))

    logits_in.wait()
    best = sweep(0, shard, 64, top_rows, jnp.full((8, tokens), LOW, F32))
    peak_here = jnp.max(best, axis=0, keepdims=True)

    def exp_rows(at, size, acc):
        part = jnp.exp(arena[pl.ds(at, size), :].astype(F32) - peak_here)
        for c in range(lane_parts):
            floats[c, pl.ds(at, size), :] = part[:, c * 128 : (c + 1) * 128]
        return acc + jnp.sum(part.reshape(size // 8, 8, tokens), axis=0)

    acc = sweep(0, shard, 64, exp_rows, jnp.zeros((8, tokens), F32))
    total_here = jnp.sum(acc, axis=0, keepdims=True)
    row8 = lax.broadcasted_iota(I32, (8, tokens), 0)
    ex1[tensor] = jnp.where(row8 == 0, peak_here, jnp.where(row8 == 1, total_here, 0.0))
    first = [
        remote(ex1.at[tensor], ex1.at[tensor], ex_send.at[0, i], ex_recv.at[0, i], group_peer(i))
        for i in range(1, PARTS)
    ]
    for copy in first:
        copy.start()

    ids = jnp.concatenate([ids_ref[...], jnp.full((PARTS, wide - block), -1, I32)], axis=1)
    local = ids - tensor * shard
    mine = (local >= 0) & (local < shard)
    own = jnp.sum(jnp.where(lax.broadcasted_iota(I32, (PARTS, wide), 0) == tensor, ids, 0), axis=0, keepdims=True)
    start = lax.broadcasted_iota(I32, (PARTS, wide), 0) * shard
    from_owner = (own >= start) & (own < start + shard)
    hits = jnp.concatenate([jnp.where(mine, 1.0, 0.0), jnp.where(from_owner, 1.0, 0.0)], axis=0)
    before = lax.broadcasted_iota(I32, (256, 256), 0)
    after = lax.broadcasted_iota(I32, (256, 256), 1)
    upper = jnp.where(before <= after, 1.0, 0.0).astype(BF16)
    seen = jnp.full((2 * PARTS, 1), -1.0, F32)
    rank_list = []
    for n in range(wide // 256):
        part = hits[:, n * 256 : (n + 1) * 256]
        rank_list.append(jnp.dot(part.astype(BF16), upper, preferred_element_type=F32) + seen)
        seen = seen + jnp.sum(part, axis=1, keepdims=True)
    ranks = jnp.concatenate(rank_list, axis=1)
    owner = lax.broadcasted_iota(I32, (PARTS, wide), 0).astype(F32) * float(slots)
    place = jnp.sum(jnp.where(from_owner, owner + ranks[PARTS:], 0.0), axis=0, keepdims=True)
    place_v[...] = jnp.clip(jnp.broadcast_to(place, (8, wide)).astype(I32), 0, PARTS * slots - 1)
    rank_v[0] = jnp.where(mine, ranks[:PARTS], -1.0)
    rank_v[1] = jnp.where(mine, local - (local & 255), 0).astype(F32)
    rank_v[2] = jnp.where(mine, local & 255, 0).astype(F32)
    to_place = pltpu.make_async_copy(place_v, place_s, s_sem.at[0])
    to_place.start()

    p1_end = p1()
    q1_end = q1()

    slot = (lax.broadcasted_iota(I32, (slots // 16, 16, wide), 0) * 16).astype(F32)
    slot = slot + lax.broadcasted_iota(I32, (slots // 16, 16, wide), 1).astype(F32)
    slot = (slot - 128.0).astype(BF16)
    kind = lax.broadcasted_iota(I32, (8, wide), 0)

    tab_v[...] = jnp.zeros_like(tab_v)

    def table_step(b, _):
        rank = jnp.minimum(rank_v[0, pl.ds(b, 1), :], float(slots)) - 128.0
        rank = jnp.broadcast_to(rank, (16, wide)).astype(BF16)
        info = jnp.where(kind == 0, rank_v[1, pl.ds(b, 1), :], jnp.where(kind == 1, rank_v[2, pl.ds(b, 1), :], 0.0))
        hot = jnp.where(slot == rank[None], jnp.ones((), BF16), jnp.zeros((), BF16)).reshape(slots, wide)
        got = lax.dot_general(info.astype(BF16), hot, NT, preferred_element_type=F32)
        found = (got[0:1, :] + got[1:2, :]).astype(I32)
        tab_v[pl.ds(b, 1), 0:slots] = jnp.clip(found, 0, shard - 1)
        return 0

    lax.fori_loop(0, two, table_step, 0)
    p1_end()
    q1_end()
    p2 = gather_ring(lambda r, h: tiles.at[0, r, pl.ds(h * two, two)], z, z_peer, 12)
    q2 = gather_ring(lambda r, h: tiles.at[1, pl.ds(h * two, two), r], y, y_peer, 18)
    lax.fori_loop(two, PARTS, table_step, 0)
    to_tab = pltpu.make_async_copy(tab_v, tab_s, s_sem.at[1])
    to_tab.start()

    for copy in first:
        copy.wait()
    peaks = [ex1[i, 0:1, :] for i in range(PARTS)]
    peak = functools.reduce(jnp.maximum, peaks)
    total = sum(ex1[i, 1:2, :] * jnp.exp(peaks[i] - peak) for i in range(PARTS))
    share = jnp.exp(peak_here - peak) / total
    to_tab.wait()
    to_place.wait()

    def pick(index_of, count):
        def go(i, _):
            got = []
            for r in range(16):
                at = index_of(i * 16 + r)
                got.append([floats[c, pl.ds(at, 1), :] for c in range(lane_parts)])
            for r in range(16):
                for c in range(lane_parts):
                    picked[c, pl.ds(i * 16 + r, 1), :] = got[r][c]
            return 0

        lax.fori_loop(0, count // 16, go, 0)

    def joined(at, size):
        return jnp.concatenate([picked[c, pl.ds(at, size), :] for c in range(lane_parts)], axis=1)

    def out_at(i):
        return arena.at[pl.ds(pl.multiple_of(i * slots, 16), slots)]

    def in_at(i):
        return arena.at[pl.ds(pl.multiple_of((PARTS + i) * slots, 16), slots)]

    def sent(i):
        to = (tensor + i) % PARTS
        return remote(out_at(to), in_at(tensor), a2a_send.at[i], a2a_recv.at[i], (dp, to))

    def pick_step(i, _):
        to = (tensor + i) % PARTS
        pick(lambda j: tab_s[to, j], slots)
        out_at(to)[...] = (joined(0, slots) * share).astype(BF16)
        return 0

    def send_step(i, _):
        sent(i).start()
        return 0

    def both_step(i, _):
        pick_step(i, 0)
        return send_step(i, 0)

    lax.fori_loop(1, HELD, pick_step, 0)
    p2_end = p2()
    q2_end = q2()
    lax.fori_loop(HELD, PARTS, pick_step, 0)
    pick(lambda j: tab_s[tensor, j], slots)
    in_at(tensor)[...] = (joined(0, slots) * share).astype(BF16)

    p2_end()
    q2_end()
    lax.fori_loop(1, PARTS, send_step, 0)
    swap_h = [
        remote(
            tiles.at[s, :, pl.ds((1 - core) * CORES, CORES)],
            tiles.at[steps, :, pl.ds(s * CORES, CORES)],
            pair_send.at[4 + s],
            pair_recv.at[4 + s],
            partner,
        )
        for s in range(steps)
    ]
    for copy in swap_h:
        copy.start()

    pieces = PARTS * sub // chunk
    each = chunk // sub
    expo[...] = jnp.zeros((rows, both), F32)

    def score_step(i, _):
        w_copy(i).wait()
        for s in range(steps):
            at = i * each
            h = tiles[s, at // RING, pl.ds(at % RING, each)].reshape(chunk, tokens)
            lanes = slice(s * tokens, (s + 1) * tokens)
            expo[0:block, lanes] += jnp.dot(w_buf[i % 2], h, preferred_element_type=F32)

        @pl.when(i + 2 < pieces)
        def _():
            w_copy(i + 2).start()

        return 0

    lax.fori_loop(0, pieces, score_step, 0)

    per = RING * sub // chunk
    count = RING * per

    def w_row(i):
        order = (2, 1, RING - 1, 0)[i // per]
        return ((z + order) % RING) * per + i % per

    def w_again(i):
        at = pl.multiple_of(w_row(i) * chunk, chunk)
        return pltpu.make_async_copy(w_ref.at[:, pl.ds(at, chunk)], w_buf.at[i % 2], w_sem.at[i % 2])

    w_again(0).start()
    w_again(1).start()
    if rows > block:
        expo[block:rows, :] = jnp.full((rows - block, both), LOW, F32)

    def top_step(at, size, m):
        return jnp.maximum(m, jnp.max(expo[pl.ds(at, size), :].reshape(size // 8, 8, both), axis=0))

    top = sweep(0, rows, 32, top_step, jnp.full((8, both), LOW, F32))
    top = jnp.max(top, axis=0, keepdims=True)

    def exp_step(at, size, a):
        value = jnp.exp(expo[pl.ds(at, size), :] - top)
        expo[pl.ds(at, size), :] = value
        return a + jnp.sum(value.reshape(size // 8, 8, both), axis=0)

    weight = sweep(0, rows, 32, exp_step, jnp.zeros((8, both), F32))
    weight = jnp.sum(weight, axis=0, keepdims=True)

    own_rows = CORES * sub
    for i in range(RING):
        for s in range(steps):
            part = tiles[s, i, pl.ds(core * CORES, CORES)].reshape(own_rows, tokens)
            hn[i, s * tokens : (s + 1) * tokens, :] = part.T
    for copy in swap_h:
        copy.wait()
    for i in range(RING):
        for s in range(steps):
            part = tiles[steps, i, s * CORES : (s + 1) * CORES].reshape(own_rows, tokens)
            hn[i, both + s * tokens : both + (s + 1) * tokens, :] = part.T

    def widen_in(i):
        part = in_at(i)[...].astype(F32)
        for c in range(lane_parts):
            floats[c, pl.ds(pl.multiple_of(i * slots, 16), slots), :] = part[:, c * 128 : (c + 1) * 128]

    widen_in(tensor)

    def arrived(i, _):
        sent(i).wait()
        widen_in((tensor + PARTS - i) % PARTS)
        return 0

    lax.fori_loop(1, PARTS, arrived, 0)
    pick(lambda j: place_s[0, j], rows)
    if rows > block:
        for c in range(lane_parts):
            picked[c, block:rows, :] = jnp.zeros((rows - block, 128), F32)

    def mass_step(at, size, a):
        return a + jnp.sum(joined(at, size).reshape(size // 8, 8, tokens), axis=0)

    mass_here = sweep(0, rows, 96, mass_step, jnp.zeros((8, tokens), F32))
    mass_here = jnp.sum(mass_here, axis=0, keepdims=True)

    row8 = lax.broadcasted_iota(I32, (8, both), 0)
    mass_wide = jnp.concatenate([mass_here] * steps, axis=1)
    ex2[tensor] = jnp.where(row8 == 0, top, jnp.where(row8 == 1, weight, jnp.where(row8 == 2, mass_wide, 0.0)))
    second = [
        remote(ex2.at[tensor], ex2.at[tensor], ex_send.at[1, i], ex_recv.at[1, i], group_peer(i))
        for i in range(1, PARTS)
    ]
    for copy in second:
        copy.start()

    scales = [LOSS_SCALE * STEP_DECAY**s for s in range(steps)]

    def shift(value, step):
        if step == 0:
            return value
        lane = lax.broadcasted_iota(I32, value.shape, 1)
        return jnp.where(lane < tokens - step, pltpu.roll(value, tokens - step, 1), 0.0)

    def shift_step(at, size, _):
        value = joined(at, size)
        for s in range(1, steps):
            moved[s - 1, pl.ds(at, size), :] = scales[s] * shift(value, s)
        return 0

    sweep(0, rows, 96, shift_step, 0)
    for copy in second:
        copy.wait()
    tops = [ex2[i, 0:1, :] for i in range(PARTS)]
    top_all = functools.reduce(jnp.maximum, tops)
    weight_all = sum(ex2[i, 1:2, :] * jnp.exp(tops[i] - top_all) for i in range(PARTS))
    mass = sum(ex2[i, 2:3, 0:tokens] for i in range(PARTS))

    factor = jnp.exp(top - top_all) / weight_all
    coefs = []
    for s in range(steps):
        mass_of = shift(jnp.broadcast_to(mass, (8, tokens)), s)[0:1, :]
        coefs.append(scales[s] * mass_of * factor[:, s * tokens : (s + 1) * tokens])

    def slope_step(at, size, _):
        for s in range(steps):
            lanes = slice(s * tokens, (s + 1) * tokens)
            prob = moved[s - 1, pl.ds(at, size), :] if s else scales[0] * joined(at, size)
            value = expo[pl.ds(at, size), lanes] * coefs[s] - prob
            sl[pl.ds(at, size), lanes] = value.astype(BF16)
        return 0

    swaps = []
    for n, (at, size) in enumerate(pieces_of(rows)):
        sweep(at, at + size, 96, slope_step, 0)
        swaps.append(
            remote(
                sl.at[pl.ds(at, size), pl.ds(0, both)],
                sl.at[pl.ds(at, size), pl.ds(both, both)],
                pair_send.at[n],
                pair_recv.at[n],
                partner,
            )
        )
        swaps[-1].start()

    def link(n, src, dst, device):
        return remote(src, dst, ring_send.at[n], ring_recv.at[n], device)

    cuts = pieces_of(rows)
    half = rows // 2

    def head_part(by, at, size):
        return jnp.dot(sl[at : at + size, :], hn[(x + by) % RING], preferred_element_type=F32)

    def x_send(slot, by, h, into, to, base, far=None, swapped=()):
        copies = []
        for n in range(2):
            at, size = cuts[2 * h + n]
            for copy in swapped[n : n + 1]:
                copy.wait()
            value = head_part(by, at, size)
            spot = pl.ds(at - h * half, size)
            if far is not None:
                value = value + x_far[far, spot, :].astype(F32)
            x_out[slot, spot, :] = value.astype(BF16)
            copies.append(link(base + n, x_out.at[slot, spot], into.at[spot], x_peer(to)))
            copies[-1].start()
        return copies

    far_r = x_send(0, 2, 0, x_far.at[0], 1, 0, swapped=swaps[:2])
    far_l = x_send(1, 2, 1, x_far.at[1], RING - 1, 2, swapped=swaps[2:])
    free_r = x_send(2, 1, 1, x_in.at[1], 1, 4)
    free_l = x_send(3, RING - 1, 0, x_in.at[2], RING - 1, 6)

    for at in range(0, rows, 128):
        size = min(128, rows - at)
        flat[:, at : at + size] = sl[at : at + size, 0:both].T

    def term_step(i):
        w_again(i).wait()
        value = jnp.dot(flat[:, 0:block], w_buf[i % 2], preferred_element_type=F32)
        first = w_row(i) * chunk
        flipped = value.T
        for lane in range(both // 128):
            spot = pl.ds(pl.multiple_of(lane % lane_parts * PARTS * sub + first, chunk), chunk)
            floats[lane // lane_parts, spot, :] = flipped[:, lane * 128 : (lane + 1) * 128]
        if i + 2 < count:
            w_again(i + 2).start()

    pair_of = RING // 2

    def spot_of(n, c, first, size):
        return pl.ds(pl.multiple_of((c * PARTS + n) * sub + first, 32), size)

    def term(s, n, first=0, size=sub):
        return jnp.concatenate([floats[s, spot_of(n, c, first, size), :] for c in range(lane_parts)], axis=1)

    def term_add(s, n, more):
        for c in range(lane_parts):
            spot = spot_of(n, c, 0, sub)
            floats[s, spot, :] = floats[s, spot, :] + more[:, c * 128 : (c + 1) * 128]

    def p_term(by, n):
        return term(0, ((z + by) % RING) * RING + n)

    def q_term(by, n):
        return term(1, n * RING + (y + by) % RING)

    class Blocks:
        def __init__(self, first, halves):
            self.first, self.halves = first, halves

        def ref(self, slot, n=None):
            if self.halves:
                at = self.first + slot // 2
                return tiles.at[at // PARTS, at // RING % RING, at % RING, pl.ds(slot % 2 * (sub // 2), sub // 2)]
            at = self.first + 2 * slot
            group = tiles.at[at // PARTS, at // RING % RING]
            return group.at[pl.ds(at % RING, 2)] if n is None else group.at[at % RING + n]

        def __getitem__(self, key):
            return self.ref(*key)[...]

    p_out, p_far, p_in = Blocks(0, False), Blocks(12, False), Blocks(16, False)
    q_out, q_far, q_in = Blocks(24, False), Blocks(36, False), Blocks(40, False)
    p2_out, p2_far, p2_in = Blocks(48, True), Blocks(51, True), Blocks(52, True)
    q2_out, q2_far, q2_in = Blocks(54, True), Blocks(57, True), Blocks(58, True)

    def ring_sum(part, out, far, into, peer, base):
        def put(slot, by, h, extra=None):
            for n, value in enumerate(part(by, h)):
                if extra is not None:
                    value = value + far[extra, n].astype(F32)
                out.ref(slot, n)[...] = value.astype(BF16)

        def start(n, slot, dst, by):
            copy = link(base + n, out.ref(slot), dst, peer(by))
            copy.start()
            return copy

        held = {}

        def begin():
            put(0, 2, 0)
            held["a"] = start(0, 0, far.ref(0), 1)
            put(1, 2, 1)
            held["b"] = start(1, 1, far.ref(1), RING - 1)

        def free():
            put(3, 1, 1)
            held["c"] = start(2, 3, into.ref(1), 1)
            put(4, RING - 1, 0)
            held["d"] = start(3, 4, into.ref(2), RING - 1)

        def late():
            held["a"].wait()
            put(2, 1, 0, 0)
            held["e"] = start(4, 2, into.ref(0), 1)
            held["b"].wait()
            put(5, RING - 1, 1, 1)
            held["f"] = start(5, 5, into.ref(3), RING - 1)

        def end():
            for name in "cdef":
                held[name].wait()

        return begin, free, late, end

    def p_part(by, h):
        return [p_term(by, h * pair_of + n) for n in range(pair_of)]

    def q_part(by, h):
        return [q_term(by, h * pair_of + n) for n in range(pair_of)]

    p_begin, p_free, p_late, p_end = ring_sum(p_part, p_out, p_far, p_in, z_peer, 12)
    q_begin, q_free, q_late, q_end = ring_sum(q_part, q_out, q_far, q_in, y_peer, 18)
    for i in range(count):
        term_step(i)
        if i + 1 == per:
            p_begin()
        if i + 1 == 3 * per:
            p_free()
    q_begin()
    q_free()
    p_late()
    q_late()

    for copy in far_r:
        copy.wait()
    dep_r = x_send(0, 1, 0, x_in.at[0], 1, 8, far=0)
    for copy in far_l:
        copy.wait()
    dep_l = x_send(1, RING - 1, 1, x_in.at[3], RING - 1, 10, far=1)

    for at, size in cuts:
        keep = min(size, block - at)
        gw_ref[at : at + keep, :] = head_part(0, at, size)[0:keep]

    p_end()
    for n in range(RING):
        got = p_in[n // pair_of, n % pair_of].astype(F32) + p_in[2 + n // pair_of, n % pair_of].astype(F32)
        term_add(0, z * RING + n, got)
    q_end()
    for n in range(RING):
        got = q_in[n // pair_of, n % pair_of].astype(F32) + q_in[2 + n // pair_of, n % pair_of].astype(F32)
        term_add(1, n * RING + y, got)

    cut = sub // 2

    def p2_part(by, h):
        return [term(0, z * RING + (y + by) % RING, h * cut, cut)]

    def q2_part(by, h):
        return [term(1, ((z + by) % RING) * RING + y, h * cut, cut)]

    p2 = ring_sum(p2_part, p2_out, p2_far, p2_in, y_peer, 24)
    q2 = ring_sum(q2_part, q2_out, q2_far, q2_in, z_peer, 30)
    for stage in range(4):
        p2[stage]()
        q2[stage]()
    for s, into in enumerate((p2_in, q2_in)):
        for h in range(2):
            value = term(s, tensor, h * cut, cut)
            value = value + into[h, 0].astype(F32) + into[2 + h, 0].astype(F32)
            gh_ref[s, h * cut : (h + 1) * cut, :] = value.astype(BF16)

    def add_in(at, size, h):
        to = at + h * half
        got = x_in[h, pl.ds(at, size), :].astype(F32) + x_in[2 + h, pl.ds(at, size), :].astype(F32)
        keep = min(size, block - to)
        gw_ref[to : to + keep, :] = gw_ref[to : to + keep, :] + got[0:keep]

    for h, from_left, from_right in ((0, dep_r, free_l), (1, free_r, dep_l)):
        for n in range(2):
            from_left[n].wait()
            from_right[n].wait()
            at, size = cuts[2 * h + n]
            for i in range(0, size, 16):
                add_in(at - h * half + i, 16, h)


def both_gradients(hid, ids, logits, w, slots):
    steps, sub, tokens = hid.shape
    parts, block = ids.shape
    shard = logits.shape[0]
    both = steps * tokens
    rows = ceil_to(block, 32)
    wide = ceil_to(block, 256)
    width = CORES * sub
    lane_parts = tokens // 128
    half = rows // 2
    depth = max(ceil_to(max(shard, parts * slots), 32), lane_parts * parts * sub)
    vmem = pl.BlockSpec(memory_space=pltpu.VMEM)
    hbm = pl.BlockSpec(memory_space=pl.ANY)
    dma = pltpu.SemaphoreType.DMA
    return pl.pallas_call(
        functools.partial(kernel, (steps, tokens, block, rows, slots)),
        out_shape=(
            jax.ShapeDtypeStruct((steps, sub, tokens), BF16),
            jax.ShapeDtypeStruct((block, width), F32),
        ),
        in_specs=[vmem, vmem, hbm, hbm],
        out_specs=(vmem, vmem),
        scratch_shapes=[
            pltpu.VMEM((2 + steps, RING, RING, sub, tokens), BF16),
            pltpu.VMEM((shard, tokens), BF16),
            pltpu.VMEM((lane_parts, depth, 128), F32),
            pltpu.VMEM((RING, CORES * both, width), BF16),
            pltpu.VMEM((rows, CORES * both), BF16),
            pltpu.VMEM((2, block, 2 * sub), BF16),
            pltpu.VMEM((lane_parts, rows, 128), F32),
            pltpu.VMEM((rows, both), F32),
            pltpu.VMEM((steps - 1, rows, tokens), F32),
            pltpu.VMEM((both, ceil_to(rows, 128)), BF16),
            pltpu.VMEM((3, parts, wide), F32),
            pltpu.VMEM((parts, ceil_to(slots, 128)), I32),
            pltpu.VMEM((8, wide), I32),
            pltpu.VMEM((parts, 8, tokens), F32),
            pltpu.VMEM((parts, 8, both), F32),
            pltpu.VMEM((4, half, width), BF16),
            pltpu.VMEM((2, half, width), BF16),
            pltpu.VMEM((4, half, width), BF16),
            pltpu.SMEM((parts, ceil_to(slots, 128)), I32),
            pltpu.SMEM((8, wide), I32),
            dma((24,)),
            dma((24,)),
            dma((parts,)),
            dma((parts,)),
            dma((2, parts)),
            dma((2, parts)),
            dma((6,)),
            dma((6,)),
            dma((2,)),
            dma((3,)),
            dma((36,)),
            dma((36,)),
        ],
        compiler_params=pltpu.CompilerParams(
            collective_id=2, has_side_effects=True, vmem_limit_bytes=63 * 2**20
        ),
        name="both_gradients",
    )(hid, ids, logits, w)


def hand_on_kernel(gh_in, gw_in, gh_out, gw_out):
    gh_out[...] = gh_in[...]
    gw_out[...] = gw_in[...]


def hand_on(gh, gw):
    steps, sub, tokens = gh.shape
    block, width = gw.shape
    blocks = 4
    size = ceil_to(-(-block // blocks), 8)
    gh_spec = pl.BlockSpec((steps, sub // blocks, tokens), lambda i: (0, i, 0))
    gw_spec = pl.BlockSpec((size, width), lambda i: (i, 0))
    return pl.pallas_call(
        hand_on_kernel,
        grid=(blocks,),
        out_shape=(jax.ShapeDtypeStruct(gh.shape, gh.dtype), jax.ShapeDtypeStruct(gw.shape, gw.dtype)),
        in_specs=[gh_spec, gw_spec],
        out_specs=(gh_spec, gw_spec),
        name="hand_on",
    )(gh, gw)


def per_device(hidden, draft_head, target_logits, draft_to_target):
    steps, tokens, _ = hidden.shape
    block = draft_to_target.shape[0] // PARTS
    heavy = block // 8
    bound = heavy + (block - heavy + PARTS - 1) // PARTS
    slots = ceil_to(bound, 16)
    w = draft_head.T
    ids = draft_to_target.reshape(PARTS, block)
    gh, gw = hand_on(*both_gradients(hidden.transpose(0, 2, 1), ids, target_logits.T, w, slots))
    return gh.transpose(0, 2, 1), gw.T


def solution(mesh):
    in_specs = (P(None, "dp", "tensor"), P(None, "tensor"), P("dp", "tensor"), P())
    out_specs = (P(None, "dp", "tensor"), P("dp", "tensor"))
    return jax.shard_map(
        per_device, mesh=mesh, in_specs=in_specs, out_specs=out_specs, check_vma=False
    )
```

time: 181 us -> 162 us (0.90)
  Pallas kernels: 173 us -> 159 us
  local copies, waits for them, and re-layouts: 7.6 us -> 1.65 us
    pallas_call x2, Pallas kernels: 173 us -> 159 us  [the longest x1 154 us: both_gradients(): pl.pallas_call(functools.partial(kernel, (steps, tokens, block, rows, slo...]
    unnamed x2 -> x0, local copies, waits for them, and re-layouts: 5.95 us -> none
where the time goes in v4:
time: 162 us; the launch traced here: 161 us
  Pallas kernels  159 us (98%)
  local copies, waits for them, and re-layouts  1.65 us (1%)
    pallas_call x1, Pallas kernels, both_gradients(): pl.pallas_call(functools.partial(kernel, (steps, tokens, block, rows, slo...  154 us
    pallas_call x1, Pallas kernels, hand_on(): pl.pallas_call(hand_on_kernel, grid=(blocks,), out_shape=(jax.ShapeDtypeS...  4.75 us

profile of v4, /device:TPU:1, one launch (start us, length us, event | category | flops | bytes accessed | tf_op | source)
XLA Modules:
  0.0 161.3 jit_solution(14382410162434255790)
XLA Ops:
  0.6 1.6 %reshape.7.ids_ref = s32[16,1500]{1,0:T(8,128)} reshape(s32[24000]{0:T(1024)} %param.7) | data formatting | bytes 192000 | tf_op jit(solution)/shard_map/reshape | solution.py:765
  2.3 154.3 %both_gradients.1 = (bf16[2,320,256]{2,1,0:T(8,128)(2,1)}, f32[1500,640]{1,0:T(8,128)}) custom-call(bf16[2,320,256]{2,1,0:T(8,128)(2,1)} %bitcast.7, s32[16,1500]{1,0:T(8,128)} %reshape.7.ids_ref, bf16[9496,256]{1,0:T(8,128)(2,1)} %bitcast.6, bf16[1500,5120]{1,0:T(8,128)(2,1)} %bitcast.5), custom_call_target="tpu_custom_call" | custom-call | tf_op jit(solution)/shard_map/both_gradients/pallas_call | solution.py:687
  156.5 4.8 %hand_on.1 = (bf16[2,320,256]{2,1,0:T(8,128)(2,1)}, f32[1500,640]{1,0:T(8,128)}) custom-call(bf16[2,320,256]{2,1,0:T(8,128)(2,1)} %get-tuple-element.6.gh_in, f32[1500,640]{1,0:T(8,128)} %get-tuple-element.7.gw_in), custom_call_target="tpu_custom_call" | custom-call | tf_op jit(solution)/shard_map/hand_on/pallas_call | solution.py:748

commit v5 on v4

--- a/solution.py
+++ b/solution.py
@@ -73,9 +73,9 @@
     w_buf,
     picked,
     expo,
-    moved,
     flat,
     rank_v,
+    count_v,
     tab_v,
     place_v,
     ex1,
@@ -218,6 +218,7 @@
         rank_list.append(jnp.dot(part.astype(BF16), upper, preferred_element_type=F32) + seen)
         seen = seen + jnp.sum(part, axis=1, keepdims=True)
     ranks = jnp.concatenate(rank_list, axis=1)
+    count_v[...] = jnp.broadcast_to(seen[:PARTS] + 1.0, count_v.shape)
     owner = lax.broadcasted_iota(I32, (PARTS, wide), 0).astype(F32) * float(slots)
     place = jnp.sum(jnp.where(from_owner, owner + ranks[PARTS:], 0.0), axis=0, keepdims=True)
     place_v[...] = jnp.clip(jnp.broadcast_to(place, (8, wide)).astype(I32), 0, PARTS * slots - 1)
@@ -265,7 +266,7 @@
     to_tab.wait()
     to_place.wait()
 
-    def pick(index_of, count):
+    def pick(index_of, first, last):
         def go(i, _):
             got = []
             for r in range(16):
@@ -276,7 +277,7 @@
                     picked[c, pl.ds(i * 16 + r, 1), :] = got[r][c]
             return 0
 
-        lax.fori_loop(0, count // 16, go, 0)
+        lax.fori_loop(first // 16, last // 16, go, 0)
 
     def joined(at, size):
         return jnp.concatenate([picked[c, pl.ds(at, size), :] for c in range(lane_parts)], axis=1)
@@ -291,26 +292,29 @@
         to = (tensor + i) % PARTS
         return remote(out_at(to), in_at(tensor), a2a_send.at[i], a2a_recv.at[i], (dp, to))
 
-    def pick_step(i, _):
+    row_of = lax.broadcasted_iota(I32, (slots, tokens), 0).astype(F32)
+
+    def pick_into(to, ref, mass):
+        pick(lambda j: tab_s[to, j], 0, slots)
+        value = (joined(0, slots) * share).astype(BF16)
+        ref[...] = value
+        used = row_of < jnp.concatenate([count_v[pl.ds(to, 1), :]] * lane_parts, axis=1)
+        value = jnp.where(used, value.astype(F32), 0.0)
+        return mass + jnp.sum(value.reshape(slots // 8, 8, tokens), axis=0)
+
+    def pick_step(i, mass):
         to = (tensor + i) % PARTS
-        pick(lambda j: tab_s[to, j], slots)
-        out_at(to)[...] = (joined(0, slots) * share).astype(BF16)
-        return 0
+        return pick_into(to, out_at(to), mass)
 
     def send_step(i, _):
         sent(i).start()
         return 0
 
-    def both_step(i, _):
-        pick_step(i, 0)
-        return send_step(i, 0)
-
-    lax.fori_loop(1, HELD, pick_step, 0)
+    mass_here = lax.fori_loop(1, HELD, pick_step, jnp.zeros((8, tokens), F32))
     p2_end = p2()
     q2_end = q2()
-    lax.fori_loop(HELD, PARTS, pick_step, 0)
-    pick(lambda j: tab_s[tensor, j], slots)
-    in_at(tensor)[...] = (joined(0, slots) * share).astype(BF16)
+    mass_here = lax.fori_loop(HELD, PARTS, pick_step, mass_here)
+    mass_here = jnp.sum(pick_into(tensor, in_at(tensor), mass_here), axis=0, keepdims=True)
 
     p2_end()
     q2_end()
@@ -390,30 +394,6 @@
             part = tiles[steps, i, s * CORES : (s + 1) * CORES].reshape(own_rows, tokens)
             hn[i, both + s * tokens : both + (s + 1) * tokens, :] = part.T
 
-    def widen_in(i):
-        part = in_at(i)[...].astype(F32)
-        for c in range(lane_parts):
-            floats[c, pl.ds(pl.multiple_of(i * slots, 16), slots), :] = part[:, c * 128 : (c + 1) * 128]
-
-    widen_in(tensor)
-
-    def arrived(i, _):
-        sent(i).wait()
-        widen_in((tensor + PARTS - i) % PARTS)
-        return 0
-
-    lax.fori_loop(1, PARTS, arrived, 0)
-    pick(lambda j: place_s[0, j], rows)
-    if rows > block:
-        for c in range(lane_parts):
-            picked[c, block:rows, :] = jnp.zeros((rows - block, 128), F32)
-
-    def mass_step(at, size, a):
-        return a + jnp.sum(joined(at, size).reshape(size // 8, 8, tokens), axis=0)
-
-    mass_here = sweep(0, rows, 96, mass_step, jnp.zeros((8, tokens), F32))
-    mass_here = jnp.sum(mass_here, axis=0, keepdims=True)
-
     row8 = lax.broadcasted_iota(I32, (8, both), 0)
     mass_wide = jnp.concatenate([mass_here] * steps, axis=1)
     ex2[tensor] = jnp.where(row8 == 0, top, jnp.where(row8 == 1, weight, jnp.where(row8 == 2, mass_wide, 0.0)))
@@ -424,21 +404,19 @@
     for copy in second:
         copy.start()
 
-    scales = [LOSS_SCALE * STEP_DECAY**s for s in range(steps)]
-
-    def shift(value, step):
-        if step == 0:
-            return value
-        lane = lax.broadcasted_iota(I32, value.shape, 1)
-        return jnp.where(lane < tokens - step, pltpu.roll(value, tokens - step, 1), 0.0)
-
-    def shift_step(at, size, _):
-        value = joined(at, size)
-        for s in range(1, steps):
-            moved[s - 1, pl.ds(at, size), :] = scales[s] * shift(value, s)
+    def widen_in(i):
+        part = in_at(i)[...].astype(F32)
+        for c in range(lane_parts):
+            floats[c, pl.ds(pl.multiple_of(i * slots, 16), slots), :] = part[:, c * 128 : (c + 1) * 128]
+
+    widen_in(tensor)
+
+    def arrived(i, _):
+        sent(i).wait()
+        widen_in((tensor + PARTS - i) % PARTS)
         return 0
 
-    sweep(0, rows, 96, shift_step, 0)
+    lax.fori_loop(1, PARTS, arrived, 0)
     for copy in second:
         copy.wait()
     tops = [ex2[i, 0:1, :] for i in range(PARTS)]
@@ -446,6 +424,14 @@
     weight_all = sum(ex2[i, 1:2, :] * jnp.exp(tops[i] - top_all) for i in range(PARTS))
     mass = sum(ex2[i, 2:3, 0:tokens] for i in range(PARTS))
 
+    scales = [LOSS_SCALE * STEP_DECAY**s for s in range(steps)]
+
+    def shift(value, step):
+        if step == 0:
+            return value
+        lane = lax.broadcasted_iota(I32, value.shape, 1)
+        return jnp.where(lane < tokens - step, pltpu.roll(value, tokens - step, 1), 0.0)
+
     factor = jnp.exp(top - top_all) / weight_all
     coefs = []
     for s in range(steps):
@@ -453,27 +439,13 @@
         coefs.append(scales[s] * mass_of * factor[:, s * tokens : (s + 1) * tokens])
 
     def slope_step(at, size, _):
+        prob = joined(at, size)
         for s in range(steps):
             lanes = slice(s * tokens, (s + 1) * tokens)
-            prob = moved[s - 1, pl.ds(at, size), :] if s else scales[0] * joined(at, size)
-            value = expo[pl.ds(at, size), lanes] * coefs[s] - prob
+            value = expo[pl.ds(at, size), lanes] * coefs[s] - scales[s] * shift(prob, s)
             sl[pl.ds(at, size), lanes] = value.astype(BF16)
         return 0
 
-    swaps = []
-    for n, (at, size) in enumerate(pieces_of(rows)):
-        sweep(at, at + size, 96, slope_step, 0)
-        swaps.append(
-            remote(
-                sl.at[pl.ds(at, size), pl.ds(0, both)],
-                sl.at[pl.ds(at, size), pl.ds(both, both)],
-                pair_send.at[n],
-                pair_recv.at[n],
-                partner,
-            )
-        )
-        swaps[-1].start()
-
     def link(n, src, dst, device):
         return remote(src, dst, ring_send.at[n], ring_recv.at[n], device)
 
@@ -483,23 +455,49 @@
     def head_part(by, at, size):
         return jnp.dot(sl[at : at + size, :], hn[(x + by) % RING], preferred_element_type=F32)
 
-    def x_send(slot, by, h, into, to, base, far=None, swapped=()):
-        copies = []
-        for n in range(2):
-            at, size = cuts[2 * h + n]
-            for copy in swapped[n : n + 1]:
-                copy.wait()
-            value = head_part(by, at, size)
-            spot = pl.ds(at - h * half, size)
-            if far is not None:
-                value = value + x_far[far, spot, :].astype(F32)
-            x_out[slot, spot, :] = value.astype(BF16)
-            copies.append(link(base + n, x_out.at[slot, spot], into.at[spot], x_peer(to)))
-            copies[-1].start()
-        return copies
-
-    far_r = x_send(0, 2, 0, x_far.at[0], 1, 0, swapped=swaps[:2])
-    far_l = x_send(1, 2, 1, x_far.at[1], RING - 1, 2, swapped=swaps[2:])
+    def x_piece(slot, by, cut, into, to, n, far=None):
+        at, size = cuts[cut]
+        value = head_part(by, at, size)
+        spot = pl.ds(at - cut // 2 * half, size)
+        if far is not None:
+            value = value + x_far[far, spot, :].astype(F32)
+        x_out[slot, spot, :] = value.astype(BF16)
+        copy = link(n, x_out.at[slot, spot], into.at[spot], x_peer(to))
+        copy.start()
+        return copy
+
+    def x_send(slot, by, h, into, to, base, far=None):
+        return [x_piece(slot, by, 2 * h + n, into, to, base + n, far) for n in range(2)]
+
+    far_of = [None] * 4
+    waiting = []
+
+    def send_far():
+        cut, copy = waiting.pop()
+        copy.wait()
+        h = cut // 2
+        far_of[cut] = x_piece(h, 2, cut, x_far.at[h], (1, RING - 1)[h], cut)
+
+    for cut in (0, 2, 1, 3):
+        at, size = cuts[cut]
+        pick(lambda j: place_s[0, j], at, at + size)
+        if at + size > block:
+            for c in range(lane_parts):
+                picked[c, block : at + size, :] = jnp.zeros((at + size - block, 128), F32)
+        sweep(at, at + size, 96, slope_step, 0)
+        swap = remote(
+            sl.at[pl.ds(at, size), pl.ds(0, both)],
+            sl.at[pl.ds(at, size), pl.ds(both, both)],
+            pair_send.at[cut],
+            pair_recv.at[cut],
+            partner,
+        )
+        swap.start()
+        if waiting:
+            send_far()
+        waiting.append((cut, swap))
+    send_far()
+    far_r, far_l = far_of[:2], far_of[2:]
     free_r = x_send(2, 1, 1, x_in.at[1], 1, 4)
     free_l = x_send(3, RING - 1, 0, x_in.at[2], RING - 1, 6)
 
@@ -701,9 +699,9 @@
             pltpu.VMEM((2, block, 2 * sub), BF16),
             pltpu.VMEM((lane_parts, rows, 128), F32),
             pltpu.VMEM((rows, both), F32),
-            pltpu.VMEM((steps - 1, rows, tokens), F32),
             pltpu.VMEM((both, ceil_to(rows, 128)), BF16),
             pltpu.VMEM((3, parts, wide), F32),
+            pltpu.VMEM((parts, 128), F32),
             pltpu.VMEM((parts, ceil_to(slots, 128)), I32),
             pltpu.VMEM((8, wide), I32),
             pltpu.VMEM((parts, 8, tokens), F32),
@@ -733,24 +731,27 @@
     )(hid, ids, logits, w)
 
 
-def hand_on_kernel(gh_in, gw_in, gh_out, gw_out):
-    gh_out[...] = gh_in[...]
-    gw_out[...] = gw_in[...]
+def hand_on_kernel(gh_in, gw_in, gh_out, gw_out, sem):
+    block = gw_in.shape[0]
+    size = ceil_to(-(-block // 4), 8)
+    copies = [pltpu.make_async_copy(gh_in, gh_out, sem.at[0])]
+    for n in range(4):
+        rows = pl.ds(n * size, min(size, block - n * size))
+        copies.append(pltpu.make_async_copy(gw_in.at[rows], gw_out.at[rows], sem.at[1 + n]))
+    for copy in copies:
+        copy.start()
+    for copy in copies:
+        copy.wait()
 
 
 def hand_on(gh, gw):
-    steps, sub, tokens = gh.shape
-    block, width = gw.shape
-    blocks = 4
-    size = ceil_to(-(-block // blocks), 8)
-    gh_spec = pl.BlockSpec((steps, sub // blocks, tokens), lambda i: (0, i, 0))
-    gw_spec = pl.BlockSpec((size, width), lambda i: (i, 0))
+    hbm = pl.BlockSpec(memory_space=pl.ANY)
     return pl.pallas_call(
         hand_on_kernel,
-        grid=(blocks,),
         out_shape=(jax.ShapeDtypeStruct(gh.shape, gh.dtype), jax.ShapeDtypeStruct(gw.shape, gw.dtype)),
-        in_specs=[gh_spec, gw_spec],
-        out_specs=(gh_spec, gw_spec),
+        in_specs=[hbm, hbm],
+        out_specs=(hbm, hbm),
+        scratch_shapes=[pltpu.SemaphoreType.DMA((5,))],
         name="hand_on",
     )(gh, gw)
 

time: 162 us -> 281 us (1.73)
  Pallas kernels: 159 us -> 278 us
    pallas_call x1, Pallas kernels: 4.75 us -> 128 us  [hand_on(): pl.pallas_call(hand_on_kernel, out_shape=(jax.ShapeDtypeStruct(gh.shape,...]
    pallas_call x1, Pallas kernels: 154 us -> 151 us  [both_gradients(): pl.pallas_call(functools.partial(kernel, (steps, tokens, block, rows, slo...]
where the time goes in v5:
time: 281 us
  Pallas kernels  278 us (99%)
    pallas_call x1, Pallas kernels, both_gradients(): pl.pallas_call(functools.partial(kernel, (steps, tokens, block, rows, slo...  151 us
    pallas_call x1, Pallas kernels, hand_on(): pl.pallas_call(hand_on_kernel, out_shape=(jax.ShapeDtypeStruct(gh.shape,...  128 us

profile of v5, /device:TPU:1, one launch (start us, length us, event | category | flops | bytes accessed | tf_op | source)
XLA Modules:
  0.0 280.9 jit_solution(4017809706807412315)
XLA Ops:
  0.6 1.6 reshape.7.ids_ref
  2.3 150.7 %both_gradients.1 = (bf16[2,320,256]{2,1,0:T(8,128)(2,1)}, f32[1500,640]{1,0:T(8,128)}) custom-call(bf16[2,320,256]{2,1,0:T(8,128)(2,1)} %bitcast.7, s32[16,1500]{1,0:T(8,128)} %reshape.7.ids_ref, bf16[9496,256]{1,0:T(8,128)(2,1)} %bitcast.6, bf16[1500,5120]{1,0:T(8,128)(2,1)} %bitcast.5), custom_call_target="tpu_custom_call" | custom-call | tf_op jit(solution)/shard_map/both_gradients/pallas_call | solution.py:685
  153.0 127.7 %hand_on.1 = (bf16[2,320,256]{2,1,0:T(8,128)(2,1)}, f32[1500,640]{1,0:T(8,128)}) custom-call(bf16[2,320,256]{2,1,0:T(8,128)(2,1)} %get-tuple-element.6.gh_in, f32[1500,640]{1,0:T(8,128)} %get-tuple-element.7.gw_in), custom_call_target="tpu_custom_call" | custom-call | tf_op jit(solution)/shard_map/hand_on/pallas_call | solution.py:749

commit v6 on v5

--- a/solution.py
+++ b/solution.py
@@ -313,12 +313,13 @@
     mass_here = lax.fori_loop(1, HELD, pick_step, jnp.zeros((8, tokens), F32))
     p2_end = p2()
     q2_end = q2()
+    lax.fori_loop(1, HELD, send_step, 0)
     mass_here = lax.fori_loop(HELD, PARTS, pick_step, mass_here)
     mass_here = jnp.sum(pick_into(tensor, in_at(tensor), mass_here), axis=0, keepdims=True)
 
     p2_end()
     q2_end()
-    lax.fori_loop(1, PARTS, send_step, 0)
+    lax.fori_loop(HELD, PARTS, send_step, 0)
     swap_h = [
         remote(
             tiles.at[s, :, pl.ds((1 - core) * CORES, CORES)],
@@ -731,17 +732,22 @@
     )(hid, ids, logits, w)
 
 
-def hand_on_kernel(gh_in, gw_in, gh_out, gw_out, sem):
+def hand_on_kernel(gh_in, gw_in, gh_out, gw_out, gh_held, gw_held, in_sem, out_sem):
     block = gw_in.shape[0]
-    size = ceil_to(-(-block // 4), 8)
-    copies = [pltpu.make_async_copy(gh_in, gh_out, sem.at[0])]
-    for n in range(4):
-        rows = pl.ds(n * size, min(size, block - n * size))
-        copies.append(pltpu.make_async_copy(gw_in.at[rows], gw_out.at[rows], sem.at[1 + n]))
-    for copy in copies:
+    size = ceil_to(-(-block // 8), 8)
+    pairs = [(gh_in, gh_held, gh_out)]
+    for at in range(0, block, size):
+        rows = pl.ds(at, min(size, block - at))
+        pairs.append((gw_in.at[rows], gw_held.at[rows], gw_out.at[rows]))
+    loads = [pltpu.make_async_copy(src, held, in_sem.at[n]) for n, (src, held, _) in enumerate(pairs)]
+    stores = [pltpu.make_async_copy(held, dst, out_sem.at[n]) for n, (_, held, dst) in enumerate(pairs)]
+    for copy in loads:
         copy.start()
-    for copy in copies:
-        copy.wait()
+    for load, store in zip(loads, stores):
+        load.wait()
+        store.start()
+    for store in stores:
+        store.wait()
 
 
 def hand_on(gh, gw):
@@ -751,7 +757,13 @@
         out_shape=(jax.ShapeDtypeStruct(gh.shape, gh.dtype), jax.ShapeDtypeStruct(gw.shape, gw.dtype)),
         in_specs=[hbm, hbm],
         out_specs=(hbm, hbm),
-        scratch_shapes=[pltpu.SemaphoreType.DMA((5,))],
+        scratch_shapes=[
+            pltpu.VMEM(gh.shape, gh.dtype),
+            pltpu.VMEM(gw.shape, gw.dtype),
+            pltpu.SemaphoreType.DMA((9,)),
+            pltpu.SemaphoreType.DMA((9,)),
+        ],
+        compiler_params=pltpu.CompilerParams(vmem_limit_bytes=50 * 2**20),
         name="hand_on",
     )(gh, gw)
 

time: 281 us -> 157 us (0.56)
  Pallas kernels: 278 us -> 153 us
    pallas_call x1, Pallas kernels: 128 us -> 3.44 us  [hand_on(): pl.pallas_call(hand_on_kernel, out_shape=(jax.ShapeDtypeStruct(gh.shape,...]
where the time goes in v6:
time: 157 us
  Pallas kernels  153 us (97%)
  local copies, waits for them, and re-layouts  2.61 us (2%)
    pallas_call x1, Pallas kernels, both_gradients(): pl.pallas_call(functools.partial(kernel, (steps, tokens, block, rows, slo...  150 us
    pallas_call x1, Pallas kernels, hand_on(): pl.pallas_call(hand_on_kernel, out_shape=(jax.ShapeDtypeStruct(gh.shape,...  3.44 us

profile of v6, /device:TPU:1, one launch (start us, length us, event | category | flops | bytes accessed | tf_op | source)
XLA Modules:
  0.0 156.9 jit_solution(14580781723184335908)
XLA Ops:
  0.6 1.6 %reshape.7.ids_ref = s32[16,1500]{1,0:T(8,128)} reshape(s32[24000]{0:T(1024)} %param.7) | data formatting | bytes 192000 | tf_op jit(solution)/shard_map/reshape | solution.py:778
  2.3 150.0 %both_gradients.1 = (bf16[2,320,256]{2,1,0:T(8,128)(2,1)}, f32[1500,640]{1,0:T(8,128)}) custom-call(bf16[2,320,256]{2,1,0:T(8,128)(2,1)} %bitcast.7, s32[16,1500]{1,0:T(8,128)} %reshape.7.ids_ref, bf16[9496,256]{1,0:T(8,128)(2,1)} %bitcast.6, bf16[1500,5120]{1,0:T(8,128)(2,1)} %bitcast.5), custom_call_target="tpu_custom_call" | custom-call | tf_op jit(solution)/shard_map/both_gradients/pallas_call | solution.py:686
  152.3 0.0 copy-start
  152.3 1.0 copy-done
  153.2 3.4 %hand_on.1 = (bf16[2,320,256]{2,1,0:T(8,128)(2,1)}, f32[1500,640]{1,0:T(8,128)}) custom-call(bf16[2,320,256]{2,1,0:T(8,128)(2,1)S(1)} %copy-done, f32[1500,640]{1,0:T(8,128)} %get-tuple-element.7.gw_in), custom_call_target="tpu_custom_call" | custom-call | tf_op jit(solution)/shard_map/hand_on/pallas_call | solution.py:755
Async XLA Ops:
  152.3 1.0 copy-start
